TPU v7x, 128 devices: a whole 4x4x4 slice. The times are simulated.
128 devices in a mesh: row: 8 (over y, core), col: 16 (over z, x).
Axes of the slice: x: 4, y: 4, z: 4, core: 2. Of those that a mesh axis runs over, the one named last changes fastest.
Arguments:
- attention_out: bfloat16 [16384, 8192], P('col', 'row'), may hold values from -6 to 6
- residual: bfloat16 [16384, 8192], P('col', 'row'), may hold values from -20 to 20
- trainer_shard: bfloat16 [8192, 8192], P(('row', 'col')), may hold values from -0.0625 to 0.0625
- norm_gain: bfloat16 [8192], P('row'), may hold values from 0.099609375 to 1.8984375
Outputs:
- served: bfloat16 [8192, 8192], P('row', 'col')
- hidden: bfloat16 [16384, 8192], P('col', 'row')
- normed: bfloat16 [16384, 8192], P('col', 'row')
All inputs are finite; a program needn't handle non-finite values.
Results may differ from a plain program's by a relative error of at most 0.0049.
Values may be sent and summed in bfloat16 or wider, within the bound.
A program may use at most 128 MiB of HBM per device.

v0:
```python
import jax
import jax.numpy as jnp
from jax import lax
from jax.sharding import PartitionSpec as P

D = 8192


def per_device(attention_out, residual, trainer_shard, norm_gain):
    gathered = lax.all_gather(attention_out, "row", axis=1, tiled=True)
    served = lax.all_to_all(trainer_shard, "col", split_axis=1, concat_axis=0, tiled=True)
    projected = lax.dot_general(
        gathered,
        lax.all_gather(served, "col", axis=1, tiled=True),
        (((1,), (1,)), ((), ())),
        preferred_element_type=jnp.float32,
    )
    hidden = (residual.astype(jnp.float32) + projected).astype(jnp.bfloat16)
    hidden_wide = hidden.astype(jnp.float32)
    squares = lax.psum(jnp.sum(hidden_wide * hidden_wide, axis=1), "row")
    mean_square = squares[:, None] / D
    normed = (
        hidden_wide * lax.rsqrt(mean_square + 1e-05) * norm_gain.astype(jnp.float32)[None, :]
    ).astype(jnp.bfloat16)
    return (served, hidden, normed)


def solution(mesh):
    in_specs = (P("col", "row"), P("col", "row"), P(("row", "col"), None), P("row"))
    out_specs = (P("row", "col"), P("col", "row"), P("col", "row"))
    return jax.shard_map(
        per_device, mesh=mesh, in_specs=in_specs, out_specs=out_specs, check_vma=False
    )
```

profile of v0, /device:TPU:1, one launch (start us, length us, event | category | flops | bytes accessed | tf_op | source)
XLA Modules:
  0.0 273.4 jit_solution(8544825445378032070)
XLA Ops:
  7.2 0.0 copy-start.1
  7.2 0.0 all-gather.3.cloned.1.call-start
  7.2 0.7 all-gather.3.cloned.1.call-update
  7.9 0.0 all-gather.5.cloned.1.call-start
  8.0 1.3 copy.13
  9.3 0.0 copy-start.2
  9.3 24.5 %all_to_all.19 = bf16[64,16,512]{2,0,1:T(8,128)(2,1)} all-to-all(bf16[64,16,512]{2,0,1:T(8,128)(2,1)S(1)} %bitcast.11), channel_id=1, replica_groups=mesh['row'=8,'col'=16] {'col'}, dimensions={1} | all-to-all | bytes 2097152 | tf_op jit(solution)/shard_map/all_to_all | solution.py:11
  33.8 0.0 all-gather.5.cloned.1.call-update
  33.8 0.0 copy-done.1
  33.8 2.6 copy.8
  36.4 0.0 copy-done.2
  36.4 61.9 %all-gather.3.cloned.1.call-done = bf16[1024,8192]{1,0:T(8,128)(2,1)} async-done(((bf16[1024,1024]{1,0:T(8,128)(2,1)}), bf16[1024,8192]{1,0:T(8,128)(2,1)}) %all-gather.3.cloned.1.call-update) | async-done | bytes 16777232 | tf_op jit(solution)/shard_map/all_gather | solution.py:10
  98.3 122.6 %all-gather.5.cloned.1.call-done = bf16[1024,8192]{1,0:T(8,128)(2,1)} async-done(((bf16[1024,512]{1,0:T(8,128)(2,1)}), bf16[1024,8192]{1,0:T(8,128)(2,1)}) %all-gather.5.cloned.1.call-update) | async-done | bytes 16777232 | tf_op jit(solution)/shard_map/all_gather | solution.py:14
  220.9 23.0 %fusion = (f32[1024]{0:T(1024)S(1)}, bf16[1024,1024]{0,1:T(8,128)(2,1)S(1)}) fusion(bf16[1024,8192]{1,0:T(8,128)(2,1)} %all-gather.3.cloned.1.call-done, bf16[1024,8192]{1,0:T(8,128)(2,1)} %all-gather.5.cloned.1.call-done, bf16[1024,1024]{0,1:T(8,128)(2,1)} %copy.8), kind=kOutput, calls=%fused_computation.2 | convolution fusion | flops 17186160640 | bytes 37752832 | tf_op jit(solution)/shard_map/dot_general | solution.py:12
  243.9 13.3 %psum.7 = f32[1024]{0:T(1024)S(1)} all-reduce(f32[1024]{0:T(1024)S(1)} %get-tuple-element.6), channel_id=1, replica_groups=mesh['row'=8,'col'=16] {'row'}, use_global_device_ids=true, to_apply=%region_1.0 | all-reduce | flops 1024 | bytes 8192 | tf_op jit(solution)/shard_map/psum | solution.py:20
  257.3 2.6 copy.9
  259.8 0.0 copy-start
  259.8 1.8 fusion.2
  261.6 3.9 %copy.10 = bf16[1024,1024]{1,0:T(8,128)(2,1)} copy(bf16[1024,1024]{0,1:T(8,128)(2,1)} %fusion.2) | data formatting | bytes 4194304
  265.6 0.0 copy-done
  265.6 1.0 copy.15
  (2 shorter events, 0.0 us)
Async XLA Ops:
  7.2 26.6 %copy-start.1 = (bf16[1024,1024]{1,0:T(8,128)(2,1)S(1)}, bf16[1024,1024]{1,0:T(8,128)(2,1)}, u32[]{:S(2)}) copy-start(bf16[1024,1024]{1,0:T(8,128)(2,1)} %param.5) | copy-start | bytes 6291460
  7.2 91.1 %all-gather.3.cloned.1.call-start = ((), (), s32[]{:S(2)}) async-start(), calls=%async_computation.1 | async-start | bytes 18874368 | tf_op jit(solution)/shard_map/all_gather | solution.py:10
  7.9 213.0 %all-gather.5.cloned.1.call-start = ((), (), s32[]{:S(2)}) async-start(), calls=%async_computation.2 | async-start | bytes 17825792 | tf_op jit(solution)/shard_map/all_gather | solution.py:14
  9.3 27.1 %copy-start.2 = (bf16[1024]{0:T(1024)(128)(2,1)S(1)}, bf16[1024]{0:T(1024)(128)(2,1)}, u32[]{:S(2)}) copy-start(bf16[1024]{0:T(1024)(128)(2,1)} %param.7) | copy-start | bytes 6148
  259.8 5.8 %copy-start = (bf16[64,16,512]{2,0,1:T(8,128)(2,1)S(1)}, bf16[64,16,512]{2,0,1:T(8,128)(2,1)}, u32[]{:S(2)}) copy-start(bf16[64,16,512]{2,0,1:T(8,128)(2,1)} %all_to_all.19) | copy-start | bytes 3145732
Sparse Core Ops, SparseCore 0:
  9.7 88.5 all-gather.2
  100.4 120.4 all-gather.4
where the time goes:
time: 274 us; the launch traced here: 273 us
  waiting for transfers between devices  185 us (68%)
  blocking collectives  37.8 us (14%)
  matrix products  23 us (8%)
  between operations  14.1 us (5%)
  local copies, waits for them, and re-layouts  11.4 us (4%)
    all_gather x1, waiting for transfers between devices, per_device(): lax.all_gather(served, 'col', axis=1, tiled=True)  123 us
    all_gather x1, waiting for transfers between devices, per_device(): gathered = lax.all_gather(attention_out, 'row', axis=1, tiled=True)  61.9 us
    all_to_all x1, blocking collectives, per_device(): lax.all_to_all(trainer_shard, 'col', split_axis=1, concat_axis=0, tiled=T...  24.5 us
    dot_general x1, matrix products, per_device(): lax.dot_general(gathered, lax.all_gather(served, 'col', axis=1, tiled=Tru...  23 us
    psum x1, blocking collectives, per_device(): squares = lax.psum(jnp.sum(hidden_wide * hidden_wide, axis=1), 'row')  13.3 us
    unnamed x10, local copies, waits for them, and re-layouts  10 us
  transfers between devices with their start and end apart: 2, of which 2 were waited for; matrix products, arithmetic and copies ran while one was open for 1% of the time, Pallas kernels for 0%

commit v1 on v0

v1 whole, which is shorter than its diff:
```python
import functools

import jax
import jax.numpy as jnp
from jax import lax
from jax.experimental import pallas as pl
from jax.experimental.pallas import tpu as pltpu
from jax.sharding import PartitionSpec as P

MESH = pl.DeviceIdType.MESH
NX = 4
NR = 8
F32 = jnp.float32
BF16 = jnp.bfloat16


def kernel(
    att, res, wsh, gain,
    served_o, hidden_o, normed_o,
    wbuf, abuf, acc, resv, hidv, normv, gainv, sums,
    w_send, w_recv, a_send, a_recv, b_send, b_recv, q_send, q_recv, l_sem,
):
    rows, kw = wsh.shape[0], abuf.shape[2]
    tokens = abuf.shape[1]
    half, quarter = rows // 2, rows // 4
    r, c = lax.axis_index("row"), lax.axis_index("col")
    my, core = r // 2, lax.rem(r, 2)
    mz, mx = c // NX, lax.rem(c, NX)

    def up(v):
        return lax.rem(v + 1, NX)

    def down(v):
        return lax.rem(v + NX - 1, NX)

    dev = [
        (r, mz * NX + up(mx)), (r, mz * NX + down(mx)),
        (r, up(mz) * NX + mx), (r, down(mz) * NX + mx),
    ]
    ydev = [(up(my) * 2 + core, c), (down(my) * 2 + core, c)]
    sibling = (my * 2 + 1 - core, c)
    peers = [(lax.rem(r + i, NR), c) for i in range(1, NR)]

    barrier = pltpu.get_barrier_semaphore()
    for d in dev + peers:
        pl.semaphore_signal(barrier, inc=1, device_id=d, device_id_type=MESH)

    def block(s):
        y = [my, up(my), down(my), lax.rem(my + 2, NX)][s // 2]
        return y * 2 + (core if s % 2 == 0 else 1 - core)

    kbs = [block(s) for s in range(NR)]

    def cols(kb):
        return pl.ds(pl.multiple_of(kb * kw, kw), kw)

    loads = {}
    def load(name, src, dst, i):
        loads[name] = pltpu.make_async_copy(src, dst, l_sem.at[i])
        loads[name].start()

    for s in range(NR):
        load("w%d" % s, wsh.at[:, cols(kbs[s])], wbuf.at[kbs[s], mz, mx], s)
    load("a", att, abuf.at[r], 8)
    load("res", res, resv, 9)
    load("gain", gain, gainv, 10)
    pl.semaphore_wait(barrier, len(dev) + len(peers))

    sent = []

    def copy(src, dst, ss, rs, d):
        return pltpu.make_async_remote_copy(
            src_ref=src, dst_ref=dst, send_sem=ss, recv_sem=rs, device_id=d, device_id_type=MESH
        )

    def go(src, dst, ss, rs, d):
        cp = copy(src, dst, ss, rs, d)
        cp.start()
        sent.append(cp)

    def w_ref(kb, h, stage, direction, sender):
        axis_x = direction < 2
        plus = direction % 2 == 0
        pos = mx if axis_x else mz
        pos = {0: pos, 1: up(pos), -1: down(pos)}[sender]
        if stage in (1, 3):
            pos = down(pos) if plus else up(pos)
        if stage < 2:
            if stage == 0:
                rs = pl.ds(h * half, half)
            else:
                rs = pl.ds(h * half + (0 if plus else quarter), quarter)
            z, x = (mz, pos) if axis_x else (pos, mx)
            return wbuf.at[kb, z, x, rs, :]
        if stage == 2:
            others = pl.ds(0, NX)
        else:
            others = pl.ds(0 if plus else NX // 2, NX // 2)
        rs = pl.ds(h * half, half)
        if axis_x:
            return wbuf.at[kb, others, pos, rs, :]
        return wbuf.at[kb, pos, others, rs, :]

    def w_dirs(stage):
        first = stage < 2
        return [(0 if (d < 2) == first else 1, d) for d in range(4)]

    def w_start(stage, s):
        for h, d in w_dirs(stage):
            ref = w_ref(kbs[s], h, stage, d, 0)
            src = ref
            if stage == 0:
                src = wsh.at[pl.ds(h * half, half), cols(kbs[s])]
            go(src, ref, w_send.at[stage, d, s], w_recv.at[stage, d, s], dev[d])

    def w_wait(stage, s):
        for h, d in w_dirs(stage):
            ref = w_ref(kbs[s], h, stage, d, -1 if d % 2 == 0 else 1)
            copy(ref, ref, w_send.at[stage, d, s], w_recv.at[stage, d, s], dev[d]).wait_recv()

    qt = tokens // 4

    def a_ref(y, q, k):
        return abuf.at[y * 2 + k, pl.ds(q * qt, qt), :]

    def a_start(hop):
        for q in range(4):
            for d in range(2):
                if hop == 0:
                    go(att.at[pl.ds(q * qt, qt), :], a_ref(my, q, core), a_send.at[0, d, q], a_recv.at[0, d, q], ydev[d])
                elif q // 2 == d:
                    ref = a_ref(down(my) if d == 0 else up(my), q, core)
                    go(ref, ref, a_send.at[1, d, q], a_recv.at[1, d, q], ydev[d])

    def a_wait(hop):
        for q in range(4):
            for d in range(2):
                if hop == 0:
                    ref = a_ref(down(my) if d == 0 else up(my), q, core)
                elif q // 2 == d:
                    ref = a_ref(lax.rem(my + 2, NX), q, core)
                else:
                    continue
                copy(ref, ref, a_send.at[hop, d, q], a_recv.at[hop, d, q], ydev[d]).wait_recv()

    def b_y(i):
        return [my, up(my), down(my), lax.rem(my + 2, NX)][i]

    def b_start(i):
        src = att if i == 0 else abuf.at[b_y(i) * 2 + core]
        go(src, abuf.at[b_y(i) * 2 + core], b_send.at[i], b_recv.at[i], sibling)

    def b_wait(i):
        ref = abuf.at[b_y(i) * 2 + 1 - core]
        copy(ref, ref, b_send.at[i], b_recv.at[i], sibling).wait_recv()

    nt = NX * rows
    def compute(s):
        kb = kbs[s]

        @pl.loop(0, NX)
        def _(z):
            w = wbuf[kb, z].reshape(nt, kw)
            at = pl.ds(pl.multiple_of(z * nt, nt), nt)
            p = lax.dot_general(abuf[kb], w, (((1,), (1,)), ((), ())), preferred_element_type=F32)
            if s == 0:
                acc[:, at] = p
            else:
                acc[:, at] += p

    a_start(0)
    for s in range(NR):
        w_start(0, s)
    b_start(0)
    for s in range(NR):
        w_wait(0, s)
        w_start(1, s)
    for s in range(NR + 2):
        if s < NR:
            w_wait(1, s)
            loads["w%d" % s].wait()
            w_start(2, s)
        if 1 <= s <= NR:
            w_wait(2, s - 1)
            w_start(3, s - 1)
        if s == 4:
            a_wait(0)
            a_start(1)
            b_start(1)
            b_start(2)
        if s == 7:
            a_wait(1)
            b_start(3)
        if s >= 2:
            w_wait(3, s - 2)
            if s == 2:
                loads["a"].wait()
            elif s == 3:
                b_wait(0)
            elif s == 5:
                b_wait(1)
            elif s == 7:
                b_wait(2)
            elif s == 9:
                b_wait(3)
            compute(s - 2)

    kb_s, part = c // 2, lax.rem(c, 2)
    served = pltpu.make_async_copy(
        wbuf.at[kb_s, :, :, :, pl.ds(pl.multiple_of(part * (kw // 2), kw // 2), kw // 2)], served_o, l_sem.at[11])
    served.start()

    loads["res"].wait()
    loads["gain"].wait()
    nb = tokens // 128
    lanes = kw // 128

    @pl.loop(0, nb)
    def _(t):
        at = pl.ds(pl.multiple_of(t * 128, 128), 128)
        h = (resv[at, :].astype(F32) + acc[at, :]).astype(BF16)
        hidv[at, :] = h
        hw = h.astype(F32)
        sq = hw * hw
        p = sq[:, 0:128]
        for i in range(1, lanes):
            p = p + sq[:, i * 128:(i + 1) * 128]
        sums[r, pl.ds(t, 1), :] = jnp.sum(p.T, axis=0, keepdims=True)

    for i, d in enumerate(peers):
        go(sums.at[r], sums.at[r], q_send.at[i], q_recv.at[i], d)
    hidden = pltpu.make_async_copy(hidv, hidden_o, l_sem.at[12])
    hidden.start()
    for i in range(1, NR):
        ref = sums.at[lax.rem(r + NR - i, NR)]
        copy(ref, ref, q_send.at[i - 1], q_recv.at[i - 1], peers[i - 1]).wait_recv()
    total = sums[0]
    for i in range(1, NR):
        total = total + sums[i]
    inv = lax.rsqrt(total / (NR * kw) + 1e-05)
    g = gainv[...].astype(F32)
    for t in range(nb):
        scale = jnp.broadcast_to(inv[t:t + 1, :], (128, 128)).T
        for i in range(lanes):
            ls = slice(i * 128, (i + 1) * 128)
            ts = slice(t * 128, (t + 1) * 128)
            normv[ts, ls] = (hidv[ts, ls].astype(F32) * scale * g[:, ls]).astype(BF16)
    normed = pltpu.make_async_copy(normv, normed_o, l_sem.at[13])
    normed.start()
    served.wait()
    hidden.wait()
    normed.wait()
    for cp in sent:
        cp.wait_send()


def per_device(attention_out, residual, trainer_shard, norm_gain):
    tokens, kw = attention_out.shape
    rows, width = trainer_shard.shape
    anywhere = pl.BlockSpec(memory_space=pl.ANY)
    dma = pltpu.SemaphoreType.DMA
    served, hidden, normed = pl.pallas_call(
        kernel,
        out_shape=(
            jax.ShapeDtypeStruct((NX, NX, rows, kw // 2), BF16),
            jax.ShapeDtypeStruct((tokens, kw), BF16),
            jax.ShapeDtypeStruct((tokens, kw), BF16),
        ),
        in_specs=[anywhere] * 4,
        out_specs=(anywhere,) * 3,
        scratch_shapes=[
            pltpu.VMEM((NR, NX, NX, rows, kw), BF16),
            pltpu.VMEM((NR, tokens, kw), BF16),
            pltpu.VMEM((tokens, kw), F32),
            pltpu.VMEM((tokens, kw), BF16),
            pltpu.VMEM((tokens, kw), BF16),
            pltpu.VMEM((tokens, kw), BF16),
            pltpu.VMEM((1, kw), BF16),
            pltpu.VMEM((NR, tokens // 128, 128), F32),
            dma((4, 4, NR)), dma((4, 4, NR)),
            dma((2, 2, 4)), dma((2, 2, 4)),
            dma((4,)), dma((4,)),
            dma((NR - 1,)), dma((NR - 1,)),
            dma((14,)),
        ],
        compiler_params=pltpu.CompilerParams(
            collective_id=0, has_side_effects=True, vmem_limit_bytes=56 * 1024 * 1024
        ),
        cost_estimate=pl.CostEstimate(
            flops=2 * tokens * kw * width, bytes_accessed=10 * tokens * kw, transcendentals=tokens
        ),
    )(attention_out, residual, trainer_shard, norm_gain.reshape(1, kw))
    return (served.reshape(NX * NX * rows, kw // 2), hidden, normed)


def solution(mesh):
    in_specs = (P("col", "row"), P("col", "row"), P(("row", "col"), None), P("row"))
    out_specs = (P("row", "col"), P("col", "row"), P("col", "row"))
    return jax.shard_map(
        per_device, mesh=mesh, in_specs=in_specs, out_specs=out_specs, check_vma=False
    )
```

time: 274 us -> 116 us (0.42)
  waiting for transfers between devices: 185 us -> 0 us
  Pallas kernels: 0 us -> 108 us
  blocking collectives: 37.8 us -> 0 us
  matrix products: 23 us -> 0 us
  between operations: 14.1 us -> 0.65 us
  local copies, waits for them, and re-layouts: 11.4 us -> 7.36 us
    all_gather x2 -> x0, waiting for transfers between devices: 185 us -> none  [the longest x1 123 us: per_device(): lax.all_gather(served, 'col', axis=1, tiled=True)]
    pallas_call x0 -> x1, Pallas kernels: none -> 108 us  [per_device(): pl.pallas_call(kernel, out_shape=(jax.ShapeDtypeStruct((NX, NX, rows, kw...]
    all_to_all x1 -> x0, blocking collectives: 24.5 us -> none  [per_device(): lax.all_to_all(trainer_shard, 'col', split_axis=1, concat_axis=0, tiled=T...]
    dot_general x1 -> x0, matrix products: 23 us -> none  [per_device(): lax.dot_general(gathered, lax.all_gather(served, 'col', axis=1, tiled=Tru...]
    psum x1 -> x0, blocking collectives: 13.3 us -> none  [per_device(): squares = lax.psum(jnp.sum(hidden_wide * hidden_wide, axis=1), 'row')]
    unnamed x10 -> x7, local copies, waits for them, and re-layouts: 10 us -> 6.08 us
  transfers between devices with their start and end apart: 2 -> 0, of which waited for: 2 -> 0; matrix products, arithmetic and copies ran while one was open for 1% -> 0% of each run, Pallas kernels for 0% -> 0%
where the time goes in v1:
time: 116 us
  Pallas kernels  108 us (93%)
  local copies, waits for them, and re-layouts  7.36 us (6%)
    pallas_call x1, Pallas kernels, per_device(): pl.pallas_call(kernel, out_shape=(jax.ShapeDtypeStruct((NX, NX, rows, kw...  108 us
    unnamed x7, local copies, waits for them, and re-layouts  6.08 us

profile of v1, /device:TPU:1, one launch (start us, length us, event | category | flops | bytes accessed | tf_op | source)
XLA Modules:
  0.0 115.6 jit_solution(6219859769191147247)
XLA Ops:
  0.6 1.3 %reshape.12.gain = bf16[1,1024]{1,0:T(2,128)(2,1)} reshape(bf16[1024]{0:T(1024)(128)(2,1)} %param.7) | data formatting | bytes 4096 | tf_op jit(solution)/shard_map/reshape | solution.py:292
  1.9 107.6 %shard_map.67 = (bf16[4,4,64,512]{3,2,1,0:T(8,128)(2,1)}, bf16[1024,1024]{1,0:T(8,128)(2,1)}, bf16[1024,1024]{1,0:T(8,128)(2,1)}) custom-call(bf16[1024,1024]{1,0:T(8,128)(2,1)} %att.1, bf16[1024,1024]{1,0:T(8,128)(2,1)} %res.1, bf16[64,8192]{1,0:T(8,128)(2,1)} %wsh.1, bf16[1,1024]{1,0:T(2,128)(2,1)} %reshape.12.gain), custom_call_target="tpu_custom_call" | custom-call | flops 17179869184 | bytes 10485760 | tf_op jit(solution)/shard_map/pallas_call | solution.py:262
  109.5 0.0 copy-start.1
  109.5 2.4 %copy.10 = bf16[1024,512]{1,0:T(8,128)(2,1)} copy(bf16[1024,512]{1,0:T(8,128)(2,1)} %bitcast.1) | data formatting | bytes 2097152
  111.9 0.0 copy-done.1
  111.9 0.0 copy-start
  111.9 1.3 %copy.11 = bf16[1024,1024]{1,0:T(8,128)(2,1)} copy(bf16[1024,1024]{1,0:T(8,128)(2,1)S(1)} %copy-done.1) | data formatting | bytes 4194304
  113.2 1.0 copy-done
  114.3 1.3 %copy.12 = bf16[1024,1024]{1,0:T(8,128)(2,1)} copy(bf16[1024,1024]{1,0:T(8,128)(2,1)S(1)} %copy-done) | data formatting | bytes 4194304
Async XLA Ops:
  109.5 2.4 %copy-start.1 = (bf16[1024,1024]{1,0:T(8,128)(2,1)S(1)}, bf16[1024,1024]{1,0:T(8,128)(2,1)}, u32[]{:S(2)}) copy-start(bf16[1024,1024]{1,0:T(8,128)(2,1)} %get-tuple-element.13) | copy-start | bytes 6291460
  111.9 2.3 %copy-start = (bf16[1024,1024]{1,0:T(8,128)(2,1)S(1)}, bf16[1024,1024]{1,0:T(8,128)(2,1)}, u32[]{:S(2)}) copy-start(bf16[1024,1024]{1,0:T(8,128)(2,1)} %get-tuple-element.14) | copy-start | bytes 6291460

commit v2 on v1

--- a/solution.py
+++ b/solution.py
@@ -15,9 +15,9 @@
 
 
 def kernel(
-    att, res, wsh, gain,
-    served_o, hidden_o, normed_o,
-    wbuf, abuf, acc, resv, hidv, normv, gainv, sums,
+    att, res, wsh,
+    served_o, hidden_o, total_o,
+    wbuf, abuf, acc, resv, squares, sums,
     w_send, w_recv, a_send, a_recv, b_send, b_recv, q_send, q_recv, l_sem,
 ):
     rows, kw = wsh.shape[0], abuf.shape[2]
@@ -63,7 +63,6 @@
         load("w%d" % s, wsh.at[:, cols(kbs[s])], wbuf.at[kbs[s], mz, mx], s)
     load("a", att, abuf.at[r], 8)
     load("res", res, resv, 9)
-    load("gain", gain, gainv, 10)
     pl.semaphore_wait(barrier, len(dev) + len(peers))
 
     sent = []
@@ -165,9 +164,19 @@
             p = lax.dot_general(abuf[kb], w, (((1,), (1,)), ((), ())), preferred_element_type=F32)
             if s == 0:
                 acc[:, at] = p
+            elif s < NR - 1:
+                acc[:, at] += p
             else:
-                acc[:, at] += p
-
+                h = (resv[:, at].astype(F32) + (acc[:, at] + p)).astype(BF16)
+                hidden_o[:, at] = h
+                hw = h.astype(F32)
+                sq = hw * hw
+                part = sq[:, 0:128]
+                for i in range(1, nt // 128):
+                    part = part + sq[:, i * 128:(i + 1) * 128]
+                squares[...] += part
+
+    squares[...] = jnp.zeros_like(squares)
     a_start(0)
     for s in range(NR):
         w_start(0, s)
@@ -203,6 +212,8 @@
                 b_wait(2)
             elif s == 9:
                 b_wait(3)
+            if s == NR + 1:
+                loads["res"].wait()
             compute(s - 2)
 
     kb_s, part = c // 2, lax.rem(c, 2)
@@ -210,86 +221,92 @@
         wbuf.at[kb_s, :, :, :, pl.ds(pl.multiple_of(part * (kw // 2), kw // 2), kw // 2)], served_o, l_sem.at[11])
     served.start()
 
-    loads["res"].wait()
-    loads["gain"].wait()
-    nb = tokens // 128
-    lanes = kw // 128
-
-    @pl.loop(0, nb)
-    def _(t):
-        at = pl.ds(pl.multiple_of(t * 128, 128), 128)
-        h = (resv[at, :].astype(F32) + acc[at, :]).astype(BF16)
-        hidv[at, :] = h
-        hw = h.astype(F32)
-        sq = hw * hw
-        p = sq[:, 0:128]
-        for i in range(1, lanes):
-            p = p + sq[:, i * 128:(i + 1) * 128]
-        sums[r, pl.ds(t, 1), :] = jnp.sum(p.T, axis=0, keepdims=True)
-
+    for t in range(tokens // 128):
+        sums[r, t:t + 1, :] = jnp.sum(squares[t * 128:(t + 1) * 128, :].T, axis=0, keepdims=True)
     for i, d in enumerate(peers):
         go(sums.at[r], sums.at[r], q_send.at[i], q_recv.at[i], d)
-    hidden = pltpu.make_async_copy(hidv, hidden_o, l_sem.at[12])
-    hidden.start()
     for i in range(1, NR):
         ref = sums.at[lax.rem(r + NR - i, NR)]
         copy(ref, ref, q_send.at[i - 1], q_recv.at[i - 1], peers[i - 1]).wait_recv()
     total = sums[0]
     for i in range(1, NR):
         total = total + sums[i]
-    inv = lax.rsqrt(total / (NR * kw) + 1e-05)
-    g = gainv[...].astype(F32)
-    for t in range(nb):
-        scale = jnp.broadcast_to(inv[t:t + 1, :], (128, 128)).T
-        for i in range(lanes):
-            ls = slice(i * 128, (i + 1) * 128)
-            ts = slice(t * 128, (t + 1) * 128)
-            normv[ts, ls] = (hidv[ts, ls].astype(F32) * scale * g[:, ls]).astype(BF16)
-    normed = pltpu.make_async_copy(normv, normed_o, l_sem.at[13])
-    normed.start()
+    total_o[...] = total
     served.wait()
-    hidden.wait()
-    normed.wait()
     for cp in sent:
         cp.wait_send()
+
+
+def finish(served, hidden, total, gain, served_o, hidden_o, normed_o, normv, sem):
+    tokens, kw = hidden.shape
+    copies = [
+        pltpu.make_async_copy(hidden, hidden_o, sem.at[0]),
+        pltpu.make_async_copy(served, served_o, sem.at[1]),
+    ]
+    for cp in copies:
+        cp.start()
+    inv = lax.rsqrt(total[...] / (NR * kw) + 1e-05)
+    g = gain[...].astype(F32)[None, :]
+    for t in range(tokens // 128):
+        ts = slice(t * 128, (t + 1) * 128)
+        scale = jnp.broadcast_to(inv[t:t + 1, :], (128, 128)).T
+        for i in range(kw // 128):
+            ls = slice(i * 128, (i + 1) * 128)
+            normv[ts, ls] = (hidden[ts, ls].astype(F32) * scale * g[:, ls]).astype(BF16)
+        cp = pltpu.make_async_copy(normv.at[ts, :], normed_o.at[ts, :], sem.at[2 + t])
+        cp.start()
+        copies.append(cp)
+    for cp in copies:
+        cp.wait()
 
 
 def per_device(attention_out, residual, trainer_shard, norm_gain):
     tokens, kw = attention_out.shape
     rows, width = trainer_shard.shape
-    anywhere = pl.BlockSpec(memory_space=pl.ANY)
+    hbm = pl.BlockSpec(memory_space=pltpu.HBM)
+    vmem = pl.BlockSpec(memory_space=pltpu.VMEM)
     dma = pltpu.SemaphoreType.DMA
-    served, hidden, normed = pl.pallas_call(
+    shapes = (
+        jax.ShapeDtypeStruct((NX, NX, rows, kw // 2), BF16),
+        jax.ShapeDtypeStruct((tokens, kw), BF16),
+        jax.ShapeDtypeStruct((tokens, kw), BF16),
+    )
+    served, hidden, total = pl.pallas_call(
         kernel,
-        out_shape=(
-            jax.ShapeDtypeStruct((NX, NX, rows, kw // 2), BF16),
-            jax.ShapeDtypeStruct((tokens, kw), BF16),
-            jax.ShapeDtypeStruct((tokens, kw), BF16),
-        ),
-        in_specs=[anywhere] * 4,
-        out_specs=(anywhere,) * 3,
+        out_shape=tuple(pltpu.VMEM(a.shape, a.dtype) for a in shapes[:2]) + (pltpu.VMEM((tokens // 128, 128), F32),),
+        in_specs=[hbm] * 3,
+        out_specs=(vmem,) * 3,
         scratch_shapes=[
             pltpu.VMEM((NR, NX, NX, rows, kw), BF16),
             pltpu.VMEM((NR, tokens, kw), BF16),
             pltpu.VMEM((tokens, kw), F32),
             pltpu.VMEM((tokens, kw), BF16),
-            pltpu.VMEM((tokens, kw), BF16),
-            pltpu.VMEM((tokens, kw), BF16),
-            pltpu.VMEM((1, kw), BF16),
+            pltpu.VMEM((tokens, 128), F32),
             pltpu.VMEM((NR, tokens // 128, 128), F32),
             dma((4, 4, NR)), dma((4, 4, NR)),
             dma((2, 2, 4)), dma((2, 2, 4)),
             dma((4,)), dma((4,)),
             dma((NR - 1,)), dma((NR - 1,)),
-            dma((14,)),
+            dma((12,)),
         ],
         compiler_params=pltpu.CompilerParams(
-            collective_id=0, has_side_effects=True, vmem_limit_bytes=56 * 1024 * 1024
+            collective_id=0, has_side_effects=True, vmem_limit_bytes=50 * 1024 * 1024
         ),
         cost_estimate=pl.CostEstimate(
-            flops=2 * tokens * kw * width, bytes_accessed=10 * tokens * kw, transcendentals=tokens
+            flops=2 * tokens * kw * width, bytes_accessed=10 * tokens * kw, transcendentals=0
         ),
-    )(attention_out, residual, trainer_shard, norm_gain.reshape(1, kw))
+    )(attention_out, residual, trainer_shard)
+    served, hidden, normed = pl.pallas_call(
+        finish,
+        out_shape=shapes,
+        in_specs=[vmem] * 4,
+        out_specs=(hbm,) * 3,
+        scratch_shapes=[pltpu.VMEM((tokens, kw), BF16), dma((2 + tokens // 128,))],
+        compiler_params=pltpu.CompilerParams(vmem_limit_bytes=16 * 1024 * 1024),
+        cost_estimate=pl.CostEstimate(
+            flops=4 * tokens * kw, bytes_accessed=5 * tokens * kw, transcendentals=tokens
+        ),
+    )(served, hidden, total, norm_gain)
     return (served.reshape(NX * NX * rows, kw // 2), hidden, normed)
 
 

time: 116 us -> 108 us (0.931)
  local copies, waits for them, and re-layouts: 7.36 us -> 0.01 us
    unnamed x7 -> x2, local copies, waits for them, and re-layouts: 6.08 us -> 0.01 us
    reshape x1 -> x0, local copies, waits for them, and re-layouts: 1.28 us -> none  [per_device(): norm_gain.reshape(1, kw)]
    pallas_call x1 -> x2, Pallas kernels: 108 us -> 107 us  [the longest x1 105 us: per_device(): pl.pallas_call(kernel, out_shape=tuple((pltpu.VMEM(a.shape, a.dtype) for...]
where the time goes in v2:
time: 108 us
  Pallas kernels  107 us (99%)
    pallas_call x1, Pallas kernels, per_device(): pl.pallas_call(kernel, out_shape=tuple((pltpu.VMEM(a.shape, a.dtype) for...  105 us
    pallas_call x1, Pallas kernels, per_device(): pl.pallas_call(finish, out_shape=shapes, in_specs=[vmem] * 4, out_specs=(...  2.41 us

profile of v2, /device:TPU:1, one launch (start us, length us, event | category | flops | bytes accessed | tf_op | source)
XLA Modules:
  0.0 108.1 jit_solution(7739655404763947845)
XLA Ops:
  0.6 0.0 copy-start
  0.6 105.0 %shard_map.67 = (bf16[4,4,64,512]{3,2,1,0:T(8,128)(2,1)S(1)}, bf16[1024,1024]{1,0:T(8,128)(2,1)S(1)}, f32[8,128]{1,0:T(8,128)S(1)}) custom-call(bf16[1024,1024]{1,0:T(8,128)(2,1)} %att.1, bf16[1024,1024]{1,0:T(8,128)(2,1)} %res.1, bf16[64,8192]{1,0:T(8,128)(2,1)} %wsh.1), custom_call_target="tpu_custom_call" | custom-call | flops 17179869184 | bytes 10485760 | tf_op jit(solution)/shard_map/pallas_call | solution.py:274
  105.7 0.0 copy-done
  105.7 2.4 %shard_map.68 = (bf16[4,4,64,512]{3,2,1,0:T(8,128)(2,1)}, bf16[1024,1024]{1,0:T(8,128)(2,1)}, bf16[1024,1024]{1,0:T(8,128)(2,1)}) custom-call(bf16[4,4,64,512]{3,2,1,0:T(8,128)(2,1)S(1)} %get-tuple-element.9.served, bf16[1024,1024]{1,0:T(8,128)(2,1)S(1)} %get-tuple-element.10.hidden, f32[8,128]{1,0:T(8,128)S(1)} %get-tuple-element.11.total, ...), custom_call_target="tpu_custom_call" | custom-call | flops 4194304 | bytes 5242880 | tf_op jit(solution)/shard_map/pallas_call | solution.py:299
Async XLA Ops:
  0.6 105.0 %copy-start = (bf16[1024]{0:T(1024)(128)(2,1)S(1)}, bf16[1024]{0:T(1024)(128)(2,1)}, u32[]{:S(2)}) copy-start(bf16[1024]{0:T(1024)(128)(2,1)} %gain.1) | copy-start | bytes 6148

commit v3 on v0

v3 whole, which is shorter than its diff:
```python
import functools

import jax
import jax.numpy as jnp
from jax import lax
from jax.experimental import pallas as pl
from jax.experimental.pallas import tpu as pltpu
from jax.sharding import PartitionSpec as P

MESH = pl.DeviceIdType.MESH
NX = 4
NR = 8
F32 = jnp.float32
BF16 = jnp.bfloat16


def level(v):
    return lax.rem(v + v // 2, 2)


def pair(v):
    return v + 1 - 2 * lax.rem(v, 2)


def mate(v):
    return NX - 1 - v


def kernel(
    att, res, wsh,
    served_o, hidden_o, total_o,
    wbuf, wother, abuf, acc, obuf, ibuf, resv, squares, sums,
    c_send, c_recv, p_send, p_recv, n_send, n_recv, y_send, y_recv, s_send, s_recv, o_send, o_recv, q_send, q_recv, l_sem,
):
    rows, kh = wsh.shape[0], abuf.shape[3]
    kw, tokens = 2 * kh, abuf.shape[2]
    part, qt = rows // 2, tokens // 4
    ht = tokens // 2
    r, c = lax.axis_index("row"), lax.axis_index("col")
    y, core = r // 2, lax.rem(r, 2)
    z, x = c // NX, lax.rem(c, NX)
    px, pz, mx, mz = pair(x), pair(z), mate(x), mate(z)
    colour = lax.rem(level(x) + level(z), 2)
    up, down, across = lax.rem(y + 1, NX), lax.rem(y + NX - 1, NX), lax.rem(y + 2, NX)

    px_dev, pz_dev, diag_dev = (r, z * NX + px), (r, pz * NX + x), (r, pz * NX + px)
    mates = [(r, z * NX + mx), (r, mz * NX + x)]
    ydev = [(up * 2 + core, c), (down * 2 + core, c)]
    sibling = (y * 2 + 1 - core, c)
    peers = [(lax.rem(r + i, NR), c) for i in range(1, NR)]

    barrier = pltpu.get_barrier_semaphore()
    greeted = [px_dev, pz_dev, diag_dev] + mates + peers
    for d in greeted:
        pl.semaphore_signal(barrier, inc=1, device_id=d, device_id_type=MESH)

    def cols(k, col):
        b = lax.rem(col + lax.rem(k, 2) + level(k // 2), 2)
        return pl.ds(pl.multiple_of(k * kw + b * kh, kh), kh)

    def my_cols(col):
        b = lax.rem(col + core + level(y), 2)
        return pl.ds(pl.multiple_of(b * kh, kh), kh)

    loads = {}

    def load(name, src, dst):
        loads[name] = pltpu.make_async_copy(src, dst, l_sem.at[len(loads)])
        loads[name].start()

    for p in range(2):
        for k in range(NR):
            ps, ks = pl.ds(p * part, part), pl.ds(k * kh, kh)
            load(("w", p, k), wsh.at[ps, cols(k, colour)], wbuf.at[z, x, ps, ks])
    for p in range(2):
        for k in range(NR):
            ps, ks = pl.ds(p * part, part), pl.ds(k * kh, kh)
            load(("v", p, k), wsh.at[ps, cols(k, 1 - colour)], wother.at[ps, ks])
    load("a", att.at[:, my_cols(colour)], abuf.at[0, r])
    load("res", res, resv)
    pl.semaphore_wait(barrier, len(greeted))

    sent = []

    def copy(src, dst, ss, rs, d):
        return pltpu.make_async_remote_copy(
            src_ref=src, dst_ref=dst, send_sem=ss, recv_sem=rs, device_id=d, device_id_type=MESH
        )

    def go(src, dst, ss, rs, d):
        cp = copy(src, dst, ss, rs, d)
        cp.start()
        sent.append(cp)

    def arrived(ref, ss, rs, d):
        copy(ref, ref, ss, rs, d).wait_recv()

    def source(at_z, at_x, s):
        return (pair(at_z) if s >= 2 else at_z), (pair(at_x) if s % 2 else at_x)

    def w_ref(at_z, at_x, s, p):
        sz, sx = source(at_z, at_x, s)
        return wbuf.at[sz, sx, pl.ds(p * part, part), :]

    def pair_start(s, p):
        ps = pl.ds(p * part, part)
        src = wbuf.at[z, x, ps, :] if s == 3 else wother.at[ps, :]
        d = [px_dev, pz_dev, diag_dev][s - 1]
        go(src, wbuf.at[z, x, ps, :], p_send.at[s - 1, p], p_recv.at[s - 1, p], d)

    def pair_wait(s, p):
        d = [px_dev, pz_dev, diag_dev][s - 1]
        arrived(w_ref(z, x, s, p), p_send.at[s - 1, p], p_recv.at[s - 1, p], d)

    def mate_start(s, p):
        i = 2 * s + p
        for l in range(2):
            ref = w_ref(z, x, s, p)
            go(ref, ref, c_send.at[l, i], c_recv.at[l, i], mates[l])

    def mate_wait(l, s, p):
        i = 2 * s + p
        ref = w_ref(z, mx, s, p) if l == 0 else w_ref(mz, x, s, p)
        arrived(ref, c_send.at[l, i], c_recv.at[l, i], mates[l])

    def forward_start(s):
        ref = w_ref(z, mx, s, 0)
        go(ref, ref, c_send.at[1, 8 + s], c_recv.at[1, 8 + s], mates[1])
        ref = w_ref(mz, x, s, 1)
        go(ref, ref, c_send.at[0, 8 + s], c_recv.at[0, 8 + s], mates[0])

    def forward_wait(s):
        for l in range(2):
            arrived(w_ref(mz, mx, s, 1 - l), c_send.at[l, 8 + s], c_recv.at[l, 8 + s], mates[l])

    chunks = [(0, 0), (1, 0), (1, ht), (0, ht)]

    def a_ref(i, at_y, k, lo, n):
        o, t0 = chunks[i]
        return abuf.at[o, at_y * 2 + k, pl.ds(t0 + lo, n), :]

    def nbr_start(i):
        o, t0 = chunks[i]
        d = pz_dev if i == 1 else px_dev
        go(att.at[pl.ds(t0, ht), my_cols(1 - colour)], a_ref(i, y, core, 0, ht), n_send.at[i - 1], n_recv.at[i - 1], d)

    def nbr_wait(i):
        d = pz_dev if i == 1 else px_dev
        arrived(a_ref(i, y, core, 0, ht), n_send.at[i - 1], n_recv.at[i - 1], d)

    def y_start(i):
        for piece in range(2):
            for d in range(2):
                lo = (piece if d == 0 else 1 - piece) * qt
                ref = a_ref(i, y, core, lo, qt)
                go(ref, ref, y_send.at[i, piece, d], y_recv.at[i, piece, d], ydev[d])

    def y_wait(i, piece):
        for d in range(2):
            lo = (piece if d == 0 else 1 - piece) * qt
            ref = a_ref(i, down if d == 0 else up, core, lo, qt)
            arrived(ref, y_send.at[i, piece, d], y_recv.at[i, piece, d], ydev[d])

    def y_forward(i):
        for d in range(2):
            ref = a_ref(i, down if d == 0 else up, core, d * qt, qt)
            go(ref, ref, y_send.at[i, 2, d], y_recv.at[i, 2, d], ydev[d])

    def y_last(i):
        for d in range(2):
            ref = a_ref(i, across, core, d * qt, qt)
            arrived(ref, y_send.at[i, 2, d], y_recv.at[i, 2, d], ydev[d])

    ys = [y, up, down, across]

    def sib_start(i, j):
        ref = a_ref(i, ys[j], core, 0, ht)
        go(ref, ref, s_send.at[i, j], s_recv.at[i, j], sibling)

    def sib_wait(i):
        for j in range(4):
            arrived(a_ref(i, ys[j], 1 - core, 0, ht), s_send.at[i, j], s_recv.at[i, j], sibling)

    nb = 2 * rows

    def blocks(i):
        qz = z + (i // 2) * (mz - z)
        qx = x + lax.rem(i, 2) * (mx - x)
        return [qz * 2 + qx // 2, pair(qz) * 2 + qx // 2]

    def product(o, t0, ns):
        w = []
        for n in ns:
            w.append(wbuf[n // 2, pl.ds(2 * lax.rem(n, 2), 2)].reshape(nb, NR * kh))
        w = w[0] if len(w) == 1 else jnp.concatenate(w, axis=0)
        a = jnp.concatenate([abuf[o, k, pl.ds(t0, ht), :] for k in range(NR)], axis=1)
        return lax.dot_general(a, w, (((1,), (1,)), ((), ())), preferred_element_type=F32)

    def out_ref(buf, h, n):
        return buf.at[n, pl.ds(h * ht, ht), :]

    def nbr_product(h, ns):
        v = product(1, h * ht, ns).astype(BF16)
        for j, n in enumerate(ns):
            obuf[n, pl.ds(h * ht, ht), :] = v[:, j * nb:(j + 1) * nb]
        for n in ns:
            copy(out_ref(obuf, h, n), out_ref(ibuf, h, n), o_send.at[h, n], o_recv.at[h, n],
                 pz_dev if h == 0 else px_dev).start()

    def own_product(h, i):
        ns = blocks(i)
        v = product(0, h * ht, ns)
        for j, n in enumerate(ns):
            ts = pl.ds(h * ht, ht)
            at = pl.ds(pl.multiple_of(n * nb, nb), nb)
            acc[n, ts, :] = v[:, j * nb:(j + 1) * nb] + resv[ts, at].astype(F32)

    for p in range(2):
        for k in range(NR):
            loads["w", p, k].wait()
        mate_start(0, p)
        if p == 0:
            nbr_start(1)
            loads["a"].wait()
            y_start(0)
    for p in range(2):
        for k in range(NR):
            loads["v", p, k].wait()
        pair_start(1, p)
        pair_start(2, p)
    sib_start(0, 0)
    pair_wait(1, 0)
    mate_start(1, 0)
    nbr_start(2)
    y_wait(0, 0)
    y_forward(0)
    pair_wait(1, 1)
    mate_start(1, 1)
    pair_start(3, 0)
    pair_start(3, 1)
    nbr_wait(1)
    y_start(1)
    sib_start(1, 0)
    y_wait(0, 1)
    sib_start(0, 1)
    sib_start(0, 2)
    pair_wait(2, 0)
    mate_start(2, 0)
    y_last(0)
    sib_start(0, 3)
    pair_wait(2, 1)
    mate_start(2, 1)
    y_wait(1, 0)
    y_forward(1)
    nbr_wait(2)
    y_start(2)
    sib_start(2, 0)
    pair_wait(3, 0)
    mate_start(3, 0)
    y_wait(1, 1)
    sib_start(1, 1)
    sib_start(1, 2)
    pair_wait(3, 1)
    mate_start(3, 1)
    y_last(1)
    sib_start(1, 3)
    for l in range(2):
        for p in range(2):
            mate_wait(l, 0, p)
    forward_start(0)
    sib_wait(0)
    loads["res"].wait()
    own_product(0, 0)
    sib_wait(1)
    nbr_product(0, blocks(0))
    y_wait(2, 0)
    y_forward(2)
    y_start(3)
    sib_start(3, 0)
    for s in (1, 2):
        for l in range(2):
            for p in range(2):
                mate_wait(l, s, p)
        forward_start(s)
    y_wait(2, 1)
    sib_start(2, 1)
    sib_start(2, 2)
    for l in range(2):
        for p in range(2):
            mate_wait(l, 3, p)
    forward_start(3)

    @pl.loop(1, 3)
    def _(i):
        nbr_product(0, blocks(i))

    y_last(2)
    sib_start(2, 3)
    forward_wait(0)
    sib_wait(2)

    @pl.loop(0, 3)
    def _(i):
        nbr_product(1, blocks(i))

    y_wait(3, 0)
    y_forward(3)
    forward_wait(1)

    @pl.loop(0, 2)
    def _(h):
        ns = blocks(3)[:1]
        v = product(1, pl.multiple_of(h * ht, ht), ns).astype(BF16)
        obuf[ns[0], pl.ds(pl.multiple_of(h * ht, ht), ht), :] = v

    n = blocks(3)[0]
    for h in range(2):
        copy(out_ref(obuf, h, n), out_ref(ibuf, h, n), o_send.at[h, n], o_recv.at[h, n], pz_dev if h == 0 else px_dev).start()

    @pl.loop(1, 3)
    def _(i):
        own_product(0, i)

    y_wait(3, 1)
    sib_start(3, 1)
    sib_start(3, 2)
    forward_wait(2)
    forward_wait(3)

    @pl.loop(0, 2)
    def _(h):
        ns = blocks(3)[1:]
        v = product(1, pl.multiple_of(h * ht, ht), ns).astype(BF16)
        obuf[ns[0], pl.ds(pl.multiple_of(h * ht, ht), ht), :] = v

    n = blocks(3)[1]
    for h in range(2):
        copy(out_ref(obuf, h, n), out_ref(ibuf, h, n), o_send.at[h, n], o_recv.at[h, n], pz_dev if h == 0 else px_dev).start()
    y_last(3)
    sib_start(3, 3)
    own_product(0, 3)
    sib_wait(3)

    @pl.loop(0, 4)
    def _(i):
        own_product(1, i)

    served = pltpu.make_async_copy(
        wbuf.at[:, :, :, pl.ds(pl.multiple_of((c // 2) * kh, kh), kh)], served_o, l_sem.at[len(loads)])
    served.start()

    squares[...] = jnp.zeros_like(squares)
    for n in range(NR):
        for h in range(2):
            arrived(out_ref(ibuf, h, n), o_send.at[h, n], o_recv.at[h, n], pz_dev if h == 0 else px_dev)

    for n in range(NR):
        h = (acc[n] + ibuf[n].astype(F32)).astype(BF16)
        hidden_o[:, n * nb:(n + 1) * nb] = h
        hw = h.astype(F32)
        squares[...] += hw * hw

    for t in range(tokens // 128):
        sums[r, t:t + 1, :] = jnp.sum(squares[t * 128:(t + 1) * 128, :].T, axis=0, keepdims=True)
    for i, d in enumerate(peers):
        go(sums.at[r], sums.at[r], q_send.at[i], q_recv.at[i], d)
    for i in range(1, NR):
        arrived(sums.at[lax.rem(r + NR - i, NR)], q_send.at[i - 1], q_recv.at[i - 1], peers[i - 1])
    total = sums[0]
    for i in range(1, NR):
        total = total + sums[i]
    total_o[...] = total
    served.wait()
    for n in range(NR):
        for h in range(2):
            copy(out_ref(obuf, h, n), out_ref(ibuf, h, n), o_send.at[h, n], o_recv.at[h, n],
                 pz_dev if h == 0 else px_dev).wait_send()
    for cp in sent:
        cp.wait_send()


def finish(served, hidden, total, gain, served_o, hidden_o, normed_o, normv, sem):
    tokens, kw = hidden.shape
    copies = [
        pltpu.make_async_copy(hidden, hidden_o, sem.at[0]),
        pltpu.make_async_copy(served, served_o, sem.at[1]),
    ]
    for cp in copies:
        cp.start()
    inv = lax.rsqrt(total[...] / (NR * kw) + 1e-05)
    g = gain[...].astype(F32)[None, :]
    for t in range(tokens // 128):
        ts = slice(t * 128, (t + 1) * 128)
        scale = jnp.broadcast_to(inv[t:t + 1, :], (128, 128)).T
        for i in range(kw // 128):
            ls = slice(i * 128, (i + 1) * 128)
            normv[ts, ls] = (hidden[ts, ls].astype(F32) * scale * g[:, ls]).astype(BF16)
        cp = pltpu.make_async_copy(normv.at[ts, :], normed_o.at[ts, :], sem.at[2 + t])
        cp.start()
        copies.append(cp)
    for cp in copies:
        cp.wait()


def per_device(attention_out, residual, trainer_shard, norm_gain):
    tokens, kw = attention_out.shape
    rows, width = trainer_shard.shape
    kh = kw // 2
    hbm = pl.BlockSpec(memory_space=pltpu.HBM)
    vmem = pl.BlockSpec(memory_space=pltpu.VMEM)
    dma = pltpu.SemaphoreType.DMA
    shapes = (
        jax.ShapeDtypeStruct((NX, NX, rows, kw // 2), BF16),
        jax.ShapeDtypeStruct((tokens, kw), BF16),
        jax.ShapeDtypeStruct((tokens, kw), BF16),
    )
    served, hidden, total = pl.pallas_call(
        kernel,
        out_shape=tuple(pltpu.VMEM(a.shape, a.dtype) for a in shapes[:2]) + (pltpu.VMEM((tokens // 128, 128), F32),),
        in_specs=[hbm] * 3,
        out_specs=(vmem,) * 3,
        scratch_shapes=[
            pltpu.VMEM((NX, NX, rows, NR * kh), BF16),
            pltpu.VMEM((rows, NR * kh), BF16),
            pltpu.VMEM((2, NR, tokens, kh), BF16),
            pltpu.VMEM((NR, tokens, 2 * rows), F32),
            pltpu.VMEM((NR, tokens, 2 * rows), BF16),
            pltpu.VMEM((NR, tokens, 2 * rows), BF16),
            pltpu.VMEM((tokens, kw), BF16),
            pltpu.VMEM((tokens, 128), F32),
            pltpu.VMEM((NR, tokens // 128, 128), F32),
            dma((2, 12)), dma((2, 12)),
            dma((3, 2)), dma((3, 2)),
            dma((2,)), dma((2,)),
            dma((4, 3, 2)), dma((4, 3, 2)),
            dma((4, 4)), dma((4, 4)),
            dma((2, NR)), dma((2, NR)),
            dma((NR - 1,)), dma((NR - 1,)),
            dma((4 * NR + 3,)),
        ],
        compiler_params=pltpu.CompilerParams(
            collective_id=0, has_side_effects=True, vmem_limit_bytes=50 * 1024 * 1024
        ),
        cost_estimate=pl.CostEstimate(
            flops=2 * tokens * kw * width, bytes_accessed=10 * tokens * kw, transcendentals=0
        ),
    )(attention_out, residual, trainer_shard)
    served, hidden, normed = pl.pallas_call(
        finish,
        out_shape=shapes,
        in_specs=[vmem] * 4,
        out_specs=(hbm,) * 3,
        scratch_shapes=[pltpu.VMEM((tokens, kw), BF16), dma((2 + tokens // 128,))],
        compiler_params=pltpu.CompilerParams(vmem_limit_bytes=16 * 1024 * 1024),
        cost_estimate=pl.CostEstimate(
            flops=4 * tokens * kw, bytes_accessed=5 * tokens * kw, transcendentals=tokens
        ),
    )(served, hidden, total, norm_gain)
    return (served.reshape(NX * NX * rows, kw // 2), hidden, normed)


def solution(mesh):
    in_specs = (P("col", "row"), P("col", "row"), P(("row", "col"), None), P("row"))
    out_specs = (P("row", "col"), P("col", "row"), P("col", "row"))
    return jax.shard_map(
        per_device, mesh=mesh, in_specs=in_specs, out_specs=out_specs, check_vma=False
    )
```

time: 274 us -> 99.9 us (0.36)
  waiting for transfers between devices: 185 us -> 0 us
  Pallas kernels: 0 us -> 99 us
  blocking collectives: 37.8 us -> 0 us
  matrix products: 23 us -> 0 us
  between operations: 14.1 us -> 0.65 us
  local copies, waits for them, and re-layouts: 11.4 us -> 0.01 us
    all_gather x2 -> x0, waiting for transfers between devices: 185 us -> none  [the longest x1 123 us: per_device(): lax.all_gather(served, 'col', axis=1, tiled=True)]
    pallas_call x0 -> x2, Pallas kernels: none -> 99 us  [the longest x1 96.5 us: per_device(): pl.pallas_call(kernel, out_shape=tuple((pltpu.VMEM(a.shape, a.dtype) for...]
    all_to_all x1 -> x0, blocking collectives: 24.5 us -> none  [per_device(): lax.all_to_all(trainer_shard, 'col', split_axis=1, concat_axis=0, tiled=T...]
    dot_general x1 -> x0, matrix products: 23 us -> none  [per_device(): lax.dot_general(gathered, lax.all_gather(served, 'col', axis=1, tiled=Tru...]
    psum x1 -> x0, blocking collectives: 13.3 us -> none  [per_device(): squares = lax.psum(jnp.sum(hidden_wide * hidden_wide, axis=1), 'row')]
    unnamed x10 -> x2, local copies, waits for them, and re-layouts: 10 us -> 0.01 us
  transfers between devices with their start and end apart: 2 -> 0, of which waited for: 2 -> 0; matrix products, arithmetic and copies ran while one was open for 1% -> 0% of each run, Pallas kernels for 0% -> 0%
where the time goes in v3:
time: 99.9 us; the launch traced here: 99.6 us
  Pallas kernels  99 us (99%)
    pallas_call x1, Pallas kernels, per_device(): pl.pallas_call(kernel, out_shape=tuple((pltpu.VMEM(a.shape, a.dtype) for...  96.5 us
    pallas_call x1, Pallas kernels, per_device(): pl.pallas_call(finish, out_shape=shapes, in_specs=[vmem] * 4, out_specs=(...  2.41 us

profile of v3, /device:TPU:1, one launch (start us, length us, event | category | flops | bytes accessed | tf_op | source)
XLA Modules:
  0.0 99.6 jit_solution(16109881884213472458)
XLA Ops:
  0.6 0.0 copy-start
  0.6 96.5 %shard_map.67 = (bf16[4,4,64,512]{3,2,1,0:T(8,128)(2,1)S(1)}, bf16[1024,1024]{1,0:T(8,128)(2,1)S(1)}, f32[8,128]{1,0:T(8,128)S(1)}) custom-call(bf16[1024,1024]{1,0:T(8,128)(2,1)} %att.1, bf16[1024,1024]{1,0:T(8,128)(2,1)} %res.1, bf16[64,8192]{1,0:T(8,128)(2,1)} %wsh.1), custom_call_target="tpu_custom_call" | custom-call | flops 17179869184 | bytes 10485760 | tf_op jit(solution)/shard_map/pallas_call | solution.py:417
  97.2 0.0 copy-done
  97.2 2.4 %shard_map.68 = (bf16[4,4,64,512]{3,2,1,0:T(8,128)(2,1)}, bf16[1024,1024]{1,0:T(8,128)(2,1)}, bf16[1024,1024]{1,0:T(8,128)(2,1)}) custom-call(bf16[4,4,64,512]{3,2,1,0:T(8,128)(2,1)S(1)} %get-tuple-element.9.served, bf16[1024,1024]{1,0:T(8,128)(2,1)S(1)} %get-tuple-element.10.hidden, f32[8,128]{1,0:T(8,128)S(1)} %get-tuple-element.11.total, ...), custom_call_target="tpu_custom_call" | custom-call | flops 4194304 | bytes 5242880 | tf_op jit(solution)/shard_map/pallas_call | solution.py:448
Async XLA Ops:
  0.6 96.6 %copy-start = (bf16[1024]{0:T(1024)(128)(2,1)S(1)}, bf16[1024]{0:T(1024)(128)(2,1)}, u32[]{:S(2)}) copy-start(bf16[1024]{0:T(1024)(128)(2,1)} %gain.1) | copy-start | bytes 6148

commit v4 on v3

--- a/solution.py
+++ b/solution.py
@@ -29,13 +29,14 @@
 def kernel(
     att, res, wsh,
     served_o, hidden_o, total_o,
-    wbuf, wother, abuf, acc, obuf, ibuf, resv, squares, sums,
+    wbuf, wother, abuf, acc, obuf, ibuf, resv, early, squares, sums,
     c_send, c_recv, p_send, p_recv, n_send, n_recv, y_send, y_recv, s_send, s_recv, o_send, o_recv, q_send, q_recv, l_sem,
 ):
     rows, kh = wsh.shape[0], abuf.shape[3]
     kw, tokens = 2 * kh, abuf.shape[2]
-    part, qt = rows // 2, tokens // 4
-    ht = tokens // 2
+    part, ht = rows // 2, tokens // 2
+    width = NR * kh
+    late = 3 * width // 4
     r, c = lax.axis_index("row"), lax.axis_index("col")
     y, core = r // 2, lax.rem(r, 2)
     z, x = c // NX, lax.rem(c, NX)
@@ -98,9 +99,9 @@
     def source(at_z, at_x, s):
         return (pair(at_z) if s >= 2 else at_z), (pair(at_x) if s % 2 else at_x)
 
-    def w_ref(at_z, at_x, s, p):
+    def w_ref(at_z, at_x, s, p, lo=0, hi=width):
         sz, sx = source(at_z, at_x, s)
-        return wbuf.at[sz, sx, pl.ds(p * part, part), :]
+        return wbuf.at[sz, sx, pl.ds(p * part, part), pl.ds(lo, hi - lo)]
 
     def pair_start(s, p):
         ps = pl.ds(p * part, part)
@@ -123,24 +124,29 @@
         ref = w_ref(z, mx, s, p) if l == 0 else w_ref(mz, x, s, p)
         arrived(ref, c_send.at[l, i], c_recv.at[l, i], mates[l])
 
-    def forward_start(s):
-        ref = w_ref(z, mx, s, 0)
-        go(ref, ref, c_send.at[1, 8 + s], c_recv.at[1, 8 + s], mates[1])
-        ref = w_ref(mz, x, s, 1)
-        go(ref, ref, c_send.at[0, 8 + s], c_recv.at[0, 8 + s], mates[0])
-
-    def forward_wait(s):
+    pieces = [(0, 0, width), (1, 0, width), (2, 0, late), (3, 0, late), (2, late, width), (3, late, width)]
+
+    def forward_start(j):
+        s, lo, hi = pieces[j]
+        ref = w_ref(z, mx, s, 0, lo, hi)
+        go(ref, ref, c_send.at[1, 8 + j], c_recv.at[1, 8 + j], mates[1])
+        ref = w_ref(mz, x, s, 1, lo, hi)
+        go(ref, ref, c_send.at[0, 8 + j], c_recv.at[0, 8 + j], mates[0])
+
+    def forward_wait(j):
+        s, lo, hi = pieces[j]
         for l in range(2):
-            arrived(w_ref(mz, mx, s, 1 - l), c_send.at[l, 8 + s], c_recv.at[l, 8 + s], mates[l])
-
-    chunks = [(0, 0), (1, 0), (1, ht), (0, ht)]
+            arrived(w_ref(mz, mx, s, 1 - l, lo, hi), c_send.at[l, 8 + j], c_recv.at[l, 8 + j], mates[l])
+
+    t1, t2 = 3 * tokens // 8, 6 * tokens // 8
+    chunks = [(0, 0, t1), (1, 0, ht), (1, ht, ht), (0, t1, t2 - t1), (0, t2, tokens - t2)]
 
     def a_ref(i, at_y, k, lo, n):
-        o, t0 = chunks[i]
+        o, t0, _ = chunks[i]
         return abuf.at[o, at_y * 2 + k, pl.ds(t0 + lo, n), :]
 
     def nbr_start(i):
-        o, t0 = chunks[i]
+        t0 = chunks[i][1]
         d = pz_dev if i == 1 else px_dev
         go(att.at[pl.ds(t0, ht), my_cols(1 - colour)], a_ref(i, y, core, 0, ht), n_send.at[i - 1], n_recv.at[i - 1], d)
 
@@ -149,71 +155,87 @@
         arrived(a_ref(i, y, core, 0, ht), n_send.at[i - 1], n_recv.at[i - 1], d)
 
     def y_start(i):
+        n = chunks[i][2] // 2
         for piece in range(2):
             for d in range(2):
-                lo = (piece if d == 0 else 1 - piece) * qt
-                ref = a_ref(i, y, core, lo, qt)
+                ref = a_ref(i, y, core, (piece if d == 0 else 1 - piece) * n, n)
                 go(ref, ref, y_send.at[i, piece, d], y_recv.at[i, piece, d], ydev[d])
 
     def y_wait(i, piece):
+        n = chunks[i][2] // 2
         for d in range(2):
-            lo = (piece if d == 0 else 1 - piece) * qt
-            ref = a_ref(i, down if d == 0 else up, core, lo, qt)
+            ref = a_ref(i, down if d == 0 else up, core, (piece if d == 0 else 1 - piece) * n, n)
             arrived(ref, y_send.at[i, piece, d], y_recv.at[i, piece, d], ydev[d])
 
     def y_forward(i):
+        n = chunks[i][2] // 2
         for d in range(2):
-            ref = a_ref(i, down if d == 0 else up, core, d * qt, qt)
+            ref = a_ref(i, down if d == 0 else up, core, d * n, n)
             go(ref, ref, y_send.at[i, 2, d], y_recv.at[i, 2, d], ydev[d])
 
     def y_last(i):
+        n = chunks[i][2] // 2
         for d in range(2):
-            ref = a_ref(i, across, core, d * qt, qt)
+            ref = a_ref(i, across, core, d * n, n)
             arrived(ref, y_send.at[i, 2, d], y_recv.at[i, 2, d], ydev[d])
 
     ys = [y, up, down, across]
 
     def sib_start(i, j):
-        ref = a_ref(i, ys[j], core, 0, ht)
+        ref = a_ref(i, ys[j], core, 0, chunks[i][2])
         go(ref, ref, s_send.at[i, j], s_recv.at[i, j], sibling)
 
-    def sib_wait(i):
-        for j in range(4):
-            arrived(a_ref(i, ys[j], 1 - core, 0, ht), s_send.at[i, j], s_recv.at[i, j], sibling)
+    def sib_wait(i, js=(0, 1, 2, 3)):
+        for j in js:
+            arrived(a_ref(i, ys[j], 1 - core, 0, chunks[i][2]), s_send.at[i, j], s_recv.at[i, j], sibling)
 
     nb = 2 * rows
 
     def blocks(i):
-        qz = z + (i // 2) * (mz - z)
-        qx = x + lax.rem(i, 2) * (mx - x)
-        return [qz * 2 + qx // 2, pair(qz) * 2 + qx // 2]
-
-    def product(o, t0, ns):
-        w = []
-        for n in ns:
-            w.append(wbuf[n // 2, pl.ds(2 * lax.rem(n, 2), 2)].reshape(nb, NR * kh))
-        w = w[0] if len(w) == 1 else jnp.concatenate(w, axis=0)
-        a = jnp.concatenate([abuf[o, k, pl.ds(t0, ht), :] for k in range(NR)], axis=1)
+        def pick(*of):
+            return jnp.where(i == 0, of[0], jnp.where(i == 1, of[1], jnp.where(i == 2, of[2], of[3])))
+
+        def block(along_z, along_x, second):
+            bz, bx = z + along_z * (mz - z), x + along_x * (mx - x)
+            return (bz + second * (pair(bz) - bz)) * 2 + bx // 2
+
+        return [
+            block(pick(0, 1, 0, 1), pick(0, 0, 1, 1), pick(0, 0, 1, 0)),
+            block(pick(0, 0, 1, 1), pick(1, 0, 0, 1), pick(0, 1, 1, 1)),
+        ]
+
+    def dot(a, w):
         return lax.dot_general(a, w, (((1,), (1,)), ((), ())), preferred_element_type=F32)
 
-    def out_ref(buf, h, n):
-        return buf.at[n, pl.ds(h * ht, ht), :]
+    def product(o, t0, nt, ns, lo=0, hi=width):
+        w = [wbuf[n // 2, pl.ds(2 * lax.rem(n, 2), 2), :, lo:hi].reshape(nb, hi - lo) for n in ns]
+        a = [abuf[o, k, pl.ds(t0, nt), :] for k in range(lo // kh, hi // kh)]
+        return dot(jnp.concatenate(a, axis=1), w[0] if len(w) == 1 else jnp.concatenate(w, axis=0))
+
+    def out_copy(h, n):
+        ts = pl.ds(h * ht, ht)
+        return copy(obuf.at[n, ts, :], ibuf.at[n, ts, :], o_send.at[h, n], o_recv.at[h, n], pz_dev if h == 0 else px_dev)
 
     def nbr_product(h, ns):
-        v = product(1, h * ht, ns).astype(BF16)
+        v = product(1, h * ht, ht, ns).astype(BF16)
         for j, n in enumerate(ns):
             obuf[n, pl.ds(h * ht, ht), :] = v[:, j * nb:(j + 1) * nb]
         for n in ns:
-            copy(out_ref(obuf, h, n), out_ref(ibuf, h, n), o_send.at[h, n], o_recv.at[h, n],
-                 pz_dev if h == 0 else px_dev).start()
-
-    def own_product(h, i):
+            out_copy(h, n).start()
+
+    def own_product(ci, i):
+        _, t0, nt = chunks[ci]
         ns = blocks(i)
-        v = product(0, h * ht, ns)
+        v = product(0, t0, nt, ns)
         for j, n in enumerate(ns):
-            ts = pl.ds(h * ht, ht)
+            ts = pl.ds(t0, nt)
             at = pl.ds(pl.multiple_of(n * nb, nb), nb)
             acc[n, ts, :] = v[:, j * nb:(j + 1) * nb] + resv[ts, at].astype(F32)
+
+    zero = r // NR
+
+    def each(lo, hi, f):
+        pl.loop(zero + lo, zero + hi)(f)
 
     for p in range(2):
         for k in range(NR):
@@ -229,11 +251,14 @@
         pair_start(1, p)
         pair_start(2, p)
     sib_start(0, 0)
+    y_wait(0, 0)
+    y_forward(0)
     pair_wait(1, 0)
     mate_start(1, 0)
     nbr_start(2)
-    y_wait(0, 0)
-    y_forward(0)
+    y_wait(0, 1)
+    sib_start(0, 1)
+    sib_start(0, 2)
     pair_wait(1, 1)
     mate_start(1, 1)
     pair_start(3, 0)
@@ -241,124 +266,134 @@
     nbr_wait(1)
     y_start(1)
     sib_start(1, 0)
-    y_wait(0, 1)
-    sib_start(0, 1)
-    sib_start(0, 2)
+    y_last(0)
+    sib_start(0, 3)
     pair_wait(2, 0)
     mate_start(2, 0)
-    y_last(0)
-    sib_start(0, 3)
+    y_wait(1, 0)
+    y_forward(1)
     pair_wait(2, 1)
     mate_start(2, 1)
-    y_wait(1, 0)
-    y_forward(1)
     nbr_wait(2)
     y_start(2)
     sib_start(2, 0)
-    pair_wait(3, 0)
-    mate_start(3, 0)
     y_wait(1, 1)
     sib_start(1, 1)
     sib_start(1, 2)
+    sib_wait(0)
+    loads["res"].wait()
+    for s in range(2):
+        for l in range(2):
+            for p in range(2):
+                mate_wait(l, s, p)
+    each(0, 1, lambda i: own_product(0, i))
+    pair_wait(3, 0)
+    mate_start(3, 0)
+    y_last(1)
+    sib_start(1, 3)
+    sib_wait(1)
+    each(0, 1, lambda i: nbr_product(0, blocks(i)))
     pair_wait(3, 1)
     mate_start(3, 1)
-    y_last(1)
-    sib_start(1, 3)
-    for l in range(2):
-        for p in range(2):
-            mate_wait(l, 0, p)
     forward_start(0)
-    sib_wait(0)
-    loads["res"].wait()
-    own_product(0, 0)
-    sib_wait(1)
-    nbr_product(0, blocks(0))
+    forward_start(1)
     y_wait(2, 0)
     y_forward(2)
     y_start(3)
     sib_start(3, 0)
-    for s in (1, 2):
-        for l in range(2):
-            for p in range(2):
-                mate_wait(l, s, p)
-        forward_start(s)
+    each(1, 2, lambda i: nbr_product(0, blocks(i)))
+    each(1, 2, lambda i: own_product(0, i))
+    for l in range(2):
+        for p in range(2):
+            mate_wait(l, 2, p)
+    forward_start(2)
     y_wait(2, 1)
     sib_start(2, 1)
     sib_start(2, 2)
     for l in range(2):
         for p in range(2):
             mate_wait(l, 3, p)
-    forward_start(3)
-
-    @pl.loop(1, 3)
-    def _(i):
-        nbr_product(0, blocks(i))
-
+    for j in range(3, 6):
+        forward_start(j)
+    each(2, 3, lambda i: nbr_product(0, blocks(i)))
     y_last(2)
     sib_start(2, 3)
-    forward_wait(0)
     sib_wait(2)
-
-    @pl.loop(0, 3)
-    def _(i):
-        nbr_product(1, blocks(i))
-
+    each(0, 2, lambda i: nbr_product(1, blocks(i)))
     y_wait(3, 0)
     y_forward(3)
-    forward_wait(1)
-
-    @pl.loop(0, 2)
-    def _(h):
-        ns = blocks(3)[:1]
-        v = product(1, pl.multiple_of(h * ht, ht), ns).astype(BF16)
-        obuf[ns[0], pl.ds(pl.multiple_of(h * ht, ht), ht), :] = v
-
-    n = blocks(3)[0]
-    for h in range(2):
-        copy(out_ref(obuf, h, n), out_ref(ibuf, h, n), o_send.at[h, n], o_recv.at[h, n], pz_dev if h == 0 else px_dev).start()
-
-    @pl.loop(1, 3)
-    def _(i):
-        own_product(0, i)
-
+    y_start(4)
+    sib_start(4, 0)
+    each(2, 3, lambda i: nbr_product(1, blocks(i)))
+    each(2, 3, lambda i: own_product(0, i))
     y_wait(3, 1)
     sib_start(3, 1)
     sib_start(3, 2)
+    forward_wait(0)
+    forward_wait(1)
+    first, last = blocks(3)
+
+    @pl.loop(0, 2)
+    def _(h):
+        ts = pl.ds(pl.multiple_of(h * ht, ht), ht)
+        obuf[first, ts, :] = product(1, ts.start, ht, [first]).astype(BF16)
+
+    for h in range(2):
+        out_copy(h, first).start()
+    y_last(3)
+    sib_start(3, 3)
+    sib_wait(3)
+    each(0, 1, lambda i: own_product(3, i))
+    y_wait(4, 0)
+    y_forward(4)
+    each(1, 3, lambda i: own_product(3, i))
     forward_wait(2)
     forward_wait(3)
 
     @pl.loop(0, 2)
     def _(h):
-        ns = blocks(3)[1:]
-        v = product(1, pl.multiple_of(h * ht, ht), ns).astype(BF16)
-        obuf[ns[0], pl.ds(pl.multiple_of(h * ht, ht), ht), :] = v
-
-    n = blocks(3)[1]
+        ts = pl.ds(pl.multiple_of(h * ht, ht), ht)
+        early[ts, :] = product(1, ts.start, ht, [last], 0, late)
+
+    y_wait(4, 1)
+    sib_start(4, 1)
+    sib_start(4, 2)
+    forward_wait(4)
+    forward_wait(5)
+
+    @pl.loop(0, 2)
+    def _(h):
+        ts = pl.ds(pl.multiple_of(h * ht, ht), ht)
+        obuf[last, ts, :] = (early[ts, :] + product(1, ts.start, ht, [last], late, width)).astype(BF16)
+
     for h in range(2):
-        copy(out_ref(obuf, h, n), out_ref(ibuf, h, n), o_send.at[h, n], o_recv.at[h, n], pz_dev if h == 0 else px_dev).start()
-    y_last(3)
-    sib_start(3, 3)
-    own_product(0, 3)
-    sib_wait(3)
-
-    @pl.loop(0, 4)
-    def _(i):
-        own_product(1, i)
+        out_copy(h, last).start()
+    y_last(4)
+    sib_start(4, 3)
+    each(3, 4, lambda i: own_product(0, i))
+    each(3, 4, lambda i: own_product(3, i))
+    sib_wait(4)
+    each(0, 4, lambda i: own_product(4, i))
 
     served = pltpu.make_async_copy(
         wbuf.at[:, :, :, pl.ds(pl.multiple_of((c // 2) * kh, kh), kh)], served_o, l_sem.at[len(loads)])
     served.start()
 
     squares[...] = jnp.zeros_like(squares)
-    for n in range(NR):
+
+    def finish_block(n):
         for h in range(2):
-            arrived(out_ref(ibuf, h, n), o_send.at[h, n], o_recv.at[h, n], pz_dev if h == 0 else px_dev)
-
-    for n in range(NR):
-        h = (acc[n] + ibuf[n].astype(F32)).astype(BF16)
-        hidden_o[:, n * nb:(n + 1) * nb] = h
-        hw = h.astype(F32)
-        squares[...] += hw * hw
+            out_copy(h, n).wait_recv()
+        hid = (acc[n] + ibuf[n].astype(F32)).astype(BF16)
+        hidden_o[:, pl.ds(pl.multiple_of(n * nb, nb), nb)] = hid
+        wide = hid.astype(F32)
+        squares[...] += wide * wide
+
+    @pl.loop(1, NR)
+    def _(i):
+        finish_block(lax.rem(last + i, NR))
+
+    finish_block(last)
 
     for t in range(tokens // 128):
         sums[r, t:t + 1, :] = jnp.sum(squares[t * 128:(t + 1) * 128, :].T, axis=0, keepdims=True)
@@ -373,8 +408,7 @@
     served.wait()
     for n in range(NR):
         for h in range(2):
-            copy(out_ref(obuf, h, n), out_ref(ibuf, h, n), o_send.at[h, n], o_recv.at[h, n],
-                 pz_dev if h == 0 else px_dev).wait_send()
+            out_copy(h, n).wait_send()
     for cp in sent:
         cp.wait_send()
 
@@ -427,13 +461,14 @@
             pltpu.VMEM((NR, tokens, 2 * rows), BF16),
             pltpu.VMEM((NR, tokens, 2 * rows), BF16),
             pltpu.VMEM((tokens, kw), BF16),
+            pltpu.VMEM((tokens, 2 * rows), F32),
             pltpu.VMEM((tokens, 128), F32),
             pltpu.VMEM((NR, tokens // 128, 128), F32),
-            dma((2, 12)), dma((2, 12)),
+            dma((2, 14)), dma((2, 14)),
             dma((3, 2)), dma((3, 2)),
             dma((2,)), dma((2,)),
-            dma((4, 3, 2)), dma((4, 3, 2)),
-            dma((4, 4)), dma((4, 4)),
+            dma((5, 3, 2)), dma((5, 3, 2)),
+            dma((5, 4)), dma((5, 4)),
             dma((2, NR)), dma((2, NR)),
             dma((NR - 1,)), dma((NR - 1,)),
             dma((4 * NR + 3,)),

time: 99.9 us -> 94.7 us (0.948)
  Pallas kernels: 99 us -> 93.8 us
    pallas_call x1, Pallas kernels: 96.5 us -> 91.3 us  [per_device(): pl.pallas_call(kernel, out_shape=tuple((pltpu.VMEM(a.shape, a.dtype) for...]
where the time goes in v4:
time: 94.7 us; the launch traced here: 94.6 us
  Pallas kernels  93.8 us (99%)
    pallas_call x1, Pallas kernels, per_device(): pl.pallas_call(kernel, out_shape=tuple((pltpu.VMEM(a.shape, a.dtype) for...  91.3 us
    pallas_call x1, Pallas kernels, per_device(): pl.pallas_call(finish, out_shape=shapes, in_specs=[vmem] * 4, out_specs=(...  2.41 us

profile of v4, /device:TPU:1, one launch (start us, length us, event | category | flops | bytes accessed | tf_op | source)
XLA Modules:
  0.0 94.6 jit_solution(1691500690918435737)
XLA Ops:
  0.6 0.0 copy-start
  0.6 91.3 %shard_map.67 = (bf16[4,4,64,512]{3,2,1,0:T(8,128)(2,1)S(1)}, bf16[1024,1024]{1,0:T(8,128)(2,1)S(1)}, f32[8,128]{1,0:T(8,128)S(1)}) custom-call(bf16[1024,1024]{1,0:T(8,128)(2,1)} %att.1, bf16[1024,1024]{1,0:T(8,128)(2,1)} %res.1, bf16[64,8192]{1,0:T(8,128)(2,1)} %wsh.1), custom_call_target="tpu_custom_call" | custom-call | flops 17179869184 | bytes 10485760 | tf_op jit(solution)/shard_map/pallas_call | solution.py:451
  92.0 0.0 copy-done
  92.0 2.4 %shard_map.68 = (bf16[4,4,64,512]{3,2,1,0:T(8,128)(2,1)}, bf16[1024,1024]{1,0:T(8,128)(2,1)}, bf16[1024,1024]{1,0:T(8,128)(2,1)}) custom-call(bf16[4,4,64,512]{3,2,1,0:T(8,128)(2,1)S(1)} %get-tuple-element.9.served, bf16[1024,1024]{1,0:T(8,128)(2,1)S(1)} %get-tuple-element.10.hidden, f32[8,128]{1,0:T(8,128)S(1)} %get-tuple-element.11.total, ...), custom_call_target="tpu_custom_call" | custom-call | flops 4194304 | bytes 5242880 | tf_op jit(solution)/shard_map/pallas_call | solution.py:483
Async XLA Ops:
  0.6 91.4 %copy-start = (bf16[1024]{0:T(1024)(128)(2,1)S(1)}, bf16[1024]{0:T(1024)(128)(2,1)}, u32[]{:S(2)}) copy-start(bf16[1024]{0:T(1024)(128)(2,1)} %gain.1) | copy-start | bytes 6148

commit v5 on v4

--- a/solution.py
+++ b/solution.py
@@ -30,7 +30,7 @@
     att, res, wsh,
     served_o, hidden_o, total_o,
     wbuf, wother, abuf, acc, obuf, ibuf, resv, early, squares, sums,
-    c_send, c_recv, p_send, p_recv, n_send, n_recv, y_send, y_recv, s_send, s_recv, o_send, o_recv, q_send, q_recv, l_sem,
+    c_send, c_recv, p_send, p_recv, n_send, n_recv, y_send, y_recv, s_send, s_recv, o_send, o_recv, q_send, q_recv, l_sem, gate,
 ):
     rows, kh = wsh.shape[0], abuf.shape[3]
     kw, tokens = 2 * kh, abuf.shape[2]
@@ -139,20 +139,22 @@
             arrived(w_ref(mz, mx, s, 1 - l, lo, hi), c_send.at[l, 8 + j], c_recv.at[l, 8 + j], mates[l])
 
     t1, t2 = 3 * tokens // 8, 6 * tokens // 8
-    chunks = [(0, 0, t1), (1, 0, ht), (1, ht, ht), (0, t1, t2 - t1), (0, t2, tokens - t2)]
+    groups = [(0, 8 * tokens // 16), (8 * tokens // 16, 8 * tokens // 16)]
+    chunks = [(0, 0, t1), (1, *groups[0]), (1, *groups[1]), (0, t1, t2 - t1), (0, t2, tokens - t2)]
 
     def a_ref(i, at_y, k, lo, n):
         o, t0, _ = chunks[i]
         return abuf.at[o, at_y * 2 + k, pl.ds(t0 + lo, n), :]
 
-    def nbr_start(i):
-        t0 = chunks[i][1]
-        d = pz_dev if i == 1 else px_dev
-        go(att.at[pl.ds(t0, ht), my_cols(1 - colour)], a_ref(i, y, core, 0, ht), n_send.at[i - 1], n_recv.at[i - 1], d)
-
-    def nbr_wait(i):
-        d = pz_dev if i == 1 else px_dev
-        arrived(a_ref(i, y, core, 0, ht), n_send.at[i - 1], n_recv.at[i - 1], d)
+    def nbr_ref(g):
+        return abuf.at[1, r, pl.ds(*groups[g]), :]
+
+    def nbr_start(g):
+        src = att.at[pl.ds(*groups[g]), my_cols(1 - colour)]
+        go(src, nbr_ref(g), n_send.at[g], n_recv.at[g], pz_dev if g == 0 else px_dev)
+
+    def nbr_wait(g):
+        arrived(nbr_ref(g), n_send.at[g], n_recv.at[g], pz_dev if g == 0 else px_dev)
 
     def y_start(i):
         n = chunks[i][2] // 2
@@ -212,26 +214,31 @@
         a = [abuf[o, k, pl.ds(t0, nt), :] for k in range(lo // kh, hi // kh)]
         return dot(jnp.concatenate(a, axis=1), w[0] if len(w) == 1 else jnp.concatenate(w, axis=0))
 
-    def out_copy(h, n):
-        ts = pl.ds(h * ht, ht)
-        return copy(obuf.at[n, ts, :], ibuf.at[n, ts, :], o_send.at[h, n], o_recv.at[h, n], pz_dev if h == 0 else px_dev)
-
-    def nbr_product(h, ns):
-        v = product(1, h * ht, ht, ns).astype(BF16)
+    def out_copy(g, n):
+        ts = pl.ds(*groups[g])
+        return copy(obuf.at[n, ts, :], ibuf.at[n, ts, :], o_send.at[g, n], o_recv.at[g, n], pz_dev if g == 0 else px_dev)
+
+    def nbr_product(g, ns):
+        v = product(1, *groups[g], ns).astype(BF16)
         for j, n in enumerate(ns):
-            obuf[n, pl.ds(h * ht, ht), :] = v[:, j * nb:(j + 1) * nb]
+            obuf[n, pl.ds(*groups[g]), :] = v[:, j * nb:(j + 1) * nb]
         for n in ns:
-            out_copy(h, n).start()
-
-    def own_product(ci, i):
-        _, t0, nt = chunks[ci]
-        ns = blocks(i)
+            out_copy(g, n).start()
+
+    def own_product(t0, nt, ns):
         v = product(0, t0, nt, ns)
         for j, n in enumerate(ns):
             ts = pl.ds(t0, nt)
             at = pl.ds(pl.multiple_of(n * nb, nb), nb)
             acc[n, ts, :] = v[:, j * nb:(j + 1) * nb] + resv[ts, at].astype(F32)
 
+    def finish(n, t0, nt):
+        ts = pl.ds(t0, nt)
+        hid = (acc[n, ts, :] + ibuf[n, ts, :].astype(F32)).astype(BF16)
+        hidden_o[ts, pl.ds(pl.multiple_of(n * nb, nb), nb)] = hid
+        wide = hid.astype(F32)
+        squares[ts, :] += wide * wide
+
     zero = r // NR
 
     def each(lo, hi, f):
@@ -242,7 +249,7 @@
             loads["w", p, k].wait()
         mate_start(0, p)
         if p == 0:
-            nbr_start(1)
+            nbr_start(0)
             loads["a"].wait()
             y_start(0)
     for p in range(2):
@@ -255,15 +262,13 @@
     y_forward(0)
     pair_wait(1, 0)
     mate_start(1, 0)
-    nbr_start(2)
+    nbr_start(1)
     y_wait(0, 1)
     sib_start(0, 1)
     sib_start(0, 2)
     pair_wait(1, 1)
     mate_start(1, 1)
-    pair_start(3, 0)
-    pair_start(3, 1)
-    nbr_wait(1)
+    nbr_wait(0)
     y_start(1)
     sib_start(1, 0)
     y_last(0)
@@ -273,20 +278,24 @@
     y_wait(1, 0)
     y_forward(1)
     pair_wait(2, 1)
+    pl.semaphore_signal(gate, inc=1, device_id=diag_dev, device_id_type=MESH)
     mate_start(2, 1)
-    nbr_wait(2)
+    nbr_wait(1)
     y_start(2)
     sib_start(2, 0)
     y_wait(1, 1)
     sib_start(1, 1)
     sib_start(1, 2)
+    pl.semaphore_wait(gate, 1)
+    pair_start(3, 0)
+    pair_start(3, 1)
     sib_wait(0)
     loads["res"].wait()
     for s in range(2):
         for l in range(2):
             for p in range(2):
                 mate_wait(l, s, p)
-    each(0, 1, lambda i: own_product(0, i))
+    each(0, 1, lambda i: own_product(0, t1, blocks(i)))
     pair_wait(3, 0)
     mate_start(3, 0)
     y_last(1)
@@ -302,7 +311,7 @@
     y_start(3)
     sib_start(3, 0)
     each(1, 2, lambda i: nbr_product(0, blocks(i)))
-    each(1, 2, lambda i: own_product(0, i))
+    each(1, 2, lambda i: own_product(0, t1, blocks(i)))
     for l in range(2):
         for p in range(2):
             mate_wait(l, 2, p)
@@ -325,10 +334,18 @@
     y_start(4)
     sib_start(4, 0)
     each(2, 3, lambda i: nbr_product(1, blocks(i)))
-    each(2, 3, lambda i: own_product(0, i))
+    each(2, 3, lambda i: own_product(0, t1, blocks(i)))
     y_wait(3, 1)
     sib_start(3, 1)
     sib_start(3, 2)
+    squares[...] = jnp.zeros_like(squares)
+
+    @pl.loop(0, 3)
+    def _(i):
+        for n in blocks(i):
+            out_copy(0, n).wait_recv()
+            finish(n, 0, t1)
+
     forward_wait(0)
     forward_wait(1)
     first, last = blocks(3)
@@ -343,10 +360,10 @@
     y_last(3)
     sib_start(3, 3)
     sib_wait(3)
-    each(0, 1, lambda i: own_product(3, i))
+    each(0, 1, lambda i: own_product(t1, t2 - t1, blocks(i)))
     y_wait(4, 0)
     y_forward(4)
-    each(1, 3, lambda i: own_product(3, i))
+    each(1, 3, lambda i: own_product(t1, t2 - t1, blocks(i)))
     forward_wait(2)
     forward_wait(3)
 
@@ -370,30 +387,24 @@
         out_copy(h, last).start()
     y_last(4)
     sib_start(4, 3)
-    each(3, 4, lambda i: own_product(0, i))
-    each(3, 4, lambda i: own_product(3, i))
+    pl.loop(0, 2)(lambda i: own_product(pl.multiple_of(i * t1, t1), t1, [first, last]))
     sib_wait(4)
-    each(0, 4, lambda i: own_product(4, i))
+    pl.loop(0, 2)(lambda i: own_product(t2, tokens - t2, blocks(2 * i) + blocks(2 * i + 1)))
 
     served = pltpu.make_async_copy(
         wbuf.at[:, :, :, pl.ds(pl.multiple_of((c // 2) * kh, kh), kh)], served_o, l_sem.at[len(loads)])
     served.start()
 
-    squares[...] = jnp.zeros_like(squares)
-
-    def finish_block(n):
-        for h in range(2):
-            out_copy(h, n).wait_recv()
-        hid = (acc[n] + ibuf[n].astype(F32)).astype(BF16)
-        hidden_o[:, pl.ds(pl.multiple_of(n * nb, nb), nb)] = hid
-        wide = hid.astype(F32)
-        squares[...] += wide * wide
-
-    @pl.loop(1, NR)
+    @pl.loop(0, 3)
     def _(i):
-        finish_block(lax.rem(last + i, NR))
-
-    finish_block(last)
+        for n in blocks(i):
+            out_copy(1, n).wait_recv()
+            finish(n, t1, tokens - t1)
+
+    for n in (first, last):
+        for g in range(2):
+            out_copy(g, n).wait_recv()
+        finish(n, 0, tokens)
 
     for t in range(tokens // 128):
         sums[r, t:t + 1, :] = jnp.sum(squares[t * 128:(t + 1) * 128, :].T, axis=0, keepdims=True)
@@ -472,6 +483,7 @@
             dma((2, NR)), dma((2, NR)),
             dma((NR - 1,)), dma((NR - 1,)),
             dma((4 * NR + 3,)),
+            pltpu.SemaphoreType.REGULAR,
         ],
         compiler_params=pltpu.CompilerParams(
             collective_id=0, has_side_effects=True, vmem_limit_bytes=50 * 1024 * 1024

time: 94.7 us -> 93.6 us (0.988)
  Pallas kernels: 93.8 us -> 92.6 us
    pallas_call x1, Pallas kernels: 91.3 us -> 90.2 us  [per_device(): pl.pallas_call(kernel, out_shape=tuple((pltpu.VMEM(a.shape, a.dtype) for...]
where the time goes in v5:
time: 93.6 us; the launch traced here: 93.5 us
  Pallas kernels  92.6 us (99%)
    pallas_call x1, Pallas kernels, per_device(): pl.pallas_call(kernel, out_shape=tuple((pltpu.VMEM(a.shape, a.dtype) for...  90.2 us
    pallas_call x1, Pallas kernels, per_device(): pl.pallas_call(finish, out_shape=shapes, in_specs=[vmem] * 4, out_specs=(...  2.41 us

profile of v5, /device:TPU:1, one launch (start us, length us, event | category | flops | bytes accessed | tf_op | source)
XLA Modules:
  0.0 93.5 jit_solution(4866706138682304184)
XLA Ops:
  0.6 0.0 copy-start
  0.6 90.2 %shard_map.67 = (bf16[4,4,64,512]{3,2,1,0:T(8,128)(2,1)S(1)}, bf16[1024,1024]{1,0:T(8,128)(2,1)S(1)}, f32[8,128]{1,0:T(8,128)S(1)}) custom-call(bf16[1024,1024]{1,0:T(8,128)(2,1)} %att.1, bf16[1024,1024]{1,0:T(8,128)(2,1)} %res.1, bf16[64,8192]{1,0:T(8,128)(2,1)} %wsh.1), custom_call_target="tpu_custom_call" | custom-call | flops 17179869184 | bytes 10485760 | tf_op jit(solution)/shard_map/pallas_call | solution.py:462
  90.9 0.0 copy-done
  90.9 2.4 %shard_map.68 = (bf16[4,4,64,512]{3,2,1,0:T(8,128)(2,1)}, bf16[1024,1024]{1,0:T(8,128)(2,1)}, bf16[1024,1024]{1,0:T(8,128)(2,1)}) custom-call(bf16[4,4,64,512]{3,2,1,0:T(8,128)(2,1)S(1)} %get-tuple-element.9.served, bf16[1024,1024]{1,0:T(8,128)(2,1)S(1)} %get-tuple-element.10.hidden, f32[8,128]{1,0:T(8,128)S(1)} %get-tuple-element.11.total, ...), custom_call_target="tpu_custom_call" | custom-call | flops 4194304 | bytes 5242880 | tf_op jit(solution)/shard_map/pallas_call | solution.py:495
Async XLA Ops:
  0.6 90.2 %copy-start = (bf16[1024]{0:T(1024)(128)(2,1)S(1)}, bf16[1024]{0:T(1024)(128)(2,1)}, u32[]{:S(2)}) copy-start(bf16[1024]{0:T(1024)(128)(2,1)} %gain.1) | copy-start | bytes 6148

commit v6 on v5

--- a/solution.py
+++ b/solution.py
@@ -63,25 +63,27 @@
         b = lax.rem(col + core + level(y), 2)
         return pl.ds(pl.multiple_of(b * kh, kh), kh)
 
-    loads = {}
-
-    def load(name, src, dst):
-        loads[name] = pltpu.make_async_copy(src, dst, l_sem.at[len(loads)])
-        loads[name].start()
+    def load(src, dst, i):
+        pltpu.make_async_copy(src, dst, l_sem.at[i]).start()
+
+    def load_wait(ref, i):
+        pltpu.make_async_copy(ref, ref, l_sem.at[i]).wait()
+
+    def load_waits(ref, i):
+        for k in range(NR):
+            load_wait(ref.at[:, pl.ds(k * kh, kh)], 7 + i * NR + k)
 
     for p in range(2):
         for k in range(NR):
             ps, ks = pl.ds(p * part, part), pl.ds(k * kh, kh)
-            load(("w", p, k), wsh.at[ps, cols(k, colour)], wbuf.at[z, x, ps, ks])
+            load(wsh.at[ps, cols(k, colour)], wbuf.at[z, x, ps, ks], 7 + p * NR + k)
     for p in range(2):
         for k in range(NR):
             ps, ks = pl.ds(p * part, part), pl.ds(k * kh, kh)
-            load(("v", p, k), wsh.at[ps, cols(k, 1 - colour)], wother.at[ps, ks])
-    load("a", att.at[:, my_cols(colour)], abuf.at[0, r])
-    load("res", res, resv)
+            load(wsh.at[ps, cols(k, 1 - colour)], wother.at[ps, ks], 7 + (2 + p) * NR + k)
+    load(att.at[:, my_cols(colour)], abuf.at[0, r], 4)
+    load(res, resv, 5)
     pl.semaphore_wait(barrier, len(greeted))
-
-    sent = []
 
     def copy(src, dst, ss, rs, d):
         return pltpu.make_async_remote_copy(
@@ -89,12 +91,13 @@
         )
 
     def go(src, dst, ss, rs, d):
-        cp = copy(src, dst, ss, rs, d)
-        cp.start()
-        sent.append(cp)
-
-    def arrived(ref, ss, rs, d):
-        copy(ref, ref, ss, rs, d).wait_recv()
+        copy(src, dst, ss, rs, d).start()
+
+    def arrived(ref, ss, rs):
+        copy(ref, ref, ss, rs, sibling).wait_recv()
+
+    def left(ref, ss, rs):
+        copy(ref, ref, ss, rs, sibling).wait_send()
 
     def source(at_z, at_x, s):
         return (pair(at_z) if s >= 2 else at_z), (pair(at_x) if s % 2 else at_x)
@@ -107,36 +110,36 @@
         ps = pl.ds(p * part, part)
         src = wbuf.at[z, x, ps, :] if s == 3 else wother.at[ps, :]
         d = [px_dev, pz_dev, diag_dev][s - 1]
-        go(src, wbuf.at[z, x, ps, :], p_send.at[s - 1, p], p_recv.at[s - 1, p], d)
+        go(src, wbuf.at[z, x, ps, :], p_send, p_recv.at[s - 1, p], d)
 
     def pair_wait(s, p):
-        d = [px_dev, pz_dev, diag_dev][s - 1]
-        arrived(w_ref(z, x, s, p), p_send.at[s - 1, p], p_recv.at[s - 1, p], d)
+        arrived(w_ref(z, x, s, p), p_send, p_recv.at[s - 1, p])
 
     def mate_start(s, p):
-        i = 2 * s + p
         for l in range(2):
             ref = w_ref(z, x, s, p)
-            go(ref, ref, c_send.at[l, i], c_recv.at[l, i], mates[l])
-
-    def mate_wait(l, s, p):
-        i = 2 * s + p
-        ref = w_ref(z, mx, s, p) if l == 0 else w_ref(mz, x, s, p)
-        arrived(ref, c_send.at[l, i], c_recv.at[l, i], mates[l])
+            go(ref, ref, c_send, c_recv.at[l, 2 * s + p], mates[l])
+
+    def mate_wait(i):
+        for s in ((0, 1), (2,), (3,))[i]:
+            for p in range(2):
+                arrived(w_ref(z, mx, s, p), c_send, c_recv.at[0, 2 * s + p])
+                arrived(w_ref(mz, x, s, p), c_send, c_recv.at[1, 2 * s + p])
 
     pieces = [(0, 0, width), (1, 0, width), (2, 0, late), (3, 0, late), (2, late, width), (3, late, width)]
 
     def forward_start(j):
         s, lo, hi = pieces[j]
         ref = w_ref(z, mx, s, 0, lo, hi)
-        go(ref, ref, c_send.at[1, 8 + j], c_recv.at[1, 8 + j], mates[1])
+        go(ref, ref, c_send, c_recv.at[1, 8 + j], mates[1])
         ref = w_ref(mz, x, s, 1, lo, hi)
-        go(ref, ref, c_send.at[0, 8 + j], c_recv.at[0, 8 + j], mates[0])
-
-    def forward_wait(j):
-        s, lo, hi = pieces[j]
-        for l in range(2):
-            arrived(w_ref(mz, mx, s, 1 - l, lo, hi), c_send.at[l, 8 + j], c_recv.at[l, 8 + j], mates[l])
+        go(ref, ref, c_send, c_recv.at[0, 8 + j], mates[0])
+
+    def forward_wait(i):
+        for j in (2 * i, 2 * i + 1):
+            s, lo, hi = pieces[j]
+            for l in range(2):
+                arrived(w_ref(mz, mx, s, 1 - l, lo, hi), c_send, c_recv.at[l, 8 + j])
 
     t1, t2 = 3 * tokens // 8, 6 * tokens // 8
     groups = [(0, 8 * tokens // 16), (8 * tokens // 16, 8 * tokens // 16)]
@@ -151,45 +154,44 @@
 
     def nbr_start(g):
         src = att.at[pl.ds(*groups[g]), my_cols(1 - colour)]
-        go(src, nbr_ref(g), n_send.at[g], n_recv.at[g], pz_dev if g == 0 else px_dev)
+        go(src, nbr_ref(g), n_send, n_recv.at[g], pz_dev if g == 0 else px_dev)
 
     def nbr_wait(g):
-        arrived(nbr_ref(g), n_send.at[g], n_recv.at[g], pz_dev if g == 0 else px_dev)
+        arrived(nbr_ref(g), n_send, n_recv.at[g])
 
     def y_start(i):
         n = chunks[i][2] // 2
         for piece in range(2):
             for d in range(2):
                 ref = a_ref(i, y, core, (piece if d == 0 else 1 - piece) * n, n)
-                go(ref, ref, y_send.at[i, piece, d], y_recv.at[i, piece, d], ydev[d])
+                go(ref, ref, y_send, y_recv.at[i, piece, d], ydev[d])
 
     def y_wait(i, piece):
         n = chunks[i][2] // 2
         for d in range(2):
             ref = a_ref(i, down if d == 0 else up, core, (piece if d == 0 else 1 - piece) * n, n)
-            arrived(ref, y_send.at[i, piece, d], y_recv.at[i, piece, d], ydev[d])
+            arrived(ref, y_send, y_recv.at[i, piece, d])
 
     def y_forward(i):
         n = chunks[i][2] // 2
         for d in range(2):
             ref = a_ref(i, down if d == 0 else up, core, d * n, n)
-            go(ref, ref, y_send.at[i, 2, d], y_recv.at[i, 2, d], ydev[d])
+            go(ref, ref, y_send, y_recv.at[i, 2, d], ydev[d])
 
     def y_last(i):
         n = chunks[i][2] // 2
         for d in range(2):
-            ref = a_ref(i, across, core, d * n, n)
-            arrived(ref, y_send.at[i, 2, d], y_recv.at[i, 2, d], ydev[d])
+            arrived(a_ref(i, across, core, d * n, n), y_send, y_recv.at[i, 2, d])
 
     ys = [y, up, down, across]
 
     def sib_start(i, j):
         ref = a_ref(i, ys[j], core, 0, chunks[i][2])
-        go(ref, ref, s_send.at[i, j], s_recv.at[i, j], sibling)
-
-    def sib_wait(i, js=(0, 1, 2, 3)):
-        for j in js:
-            arrived(a_ref(i, ys[j], 1 - core, 0, chunks[i][2]), s_send.at[i, j], s_recv.at[i, j], sibling)
+        go(ref, ref, s_send, s_recv.at[i, j], sibling)
+
+    def sib_wait(i):
+        for j in range(4):
+            arrived(a_ref(i, ys[j], 1 - core, 0, chunks[i][2]), s_send, s_recv.at[i, j])
 
     nb = 2 * rows
 
@@ -214,16 +216,19 @@
         a = [abuf[o, k, pl.ds(t0, nt), :] for k in range(lo // kh, hi // kh)]
         return dot(jnp.concatenate(a, axis=1), w[0] if len(w) == 1 else jnp.concatenate(w, axis=0))
 
-    def out_copy(g, n):
+    def out_start(g, n):
         ts = pl.ds(*groups[g])
-        return copy(obuf.at[n, ts, :], ibuf.at[n, ts, :], o_send.at[g, n], o_recv.at[g, n], pz_dev if g == 0 else px_dev)
+        go(obuf.at[n, ts, :], ibuf.at[n, ts, :], o_send, o_recv.at[g, n], pz_dev if g == 0 else px_dev)
+
+    def out_wait(g, n):
+        arrived(ibuf.at[n, pl.ds(*groups[g]), :], o_send, o_recv.at[g, n])
 
     def nbr_product(g, ns):
         v = product(1, *groups[g], ns).astype(BF16)
         for j, n in enumerate(ns):
             obuf[n, pl.ds(*groups[g]), :] = v[:, j * nb:(j + 1) * nb]
         for n in ns:
-            out_copy(g, n).start()
+            out_start(g, n)
 
     def own_product(t0, nt, ns):
         v = product(0, t0, nt, ns)
@@ -245,16 +250,14 @@
         pl.loop(zero + lo, zero + hi)(f)
 
     for p in range(2):
-        for k in range(NR):
-            loads["w", p, k].wait()
+        load_waits(wbuf.at[z, x, pl.ds(p * part, part), :], p)
         mate_start(0, p)
         if p == 0:
             nbr_start(0)
-            loads["a"].wait()
+            load_wait(abuf.at[0, r], 4)
             y_start(0)
     for p in range(2):
-        for k in range(NR):
-            loads["v", p, k].wait()
+        load_waits(wother.at[pl.ds(p * part, part), :], 2 + p)
         pair_start(1, p)
         pair_start(2, p)
     sib_start(0, 0)
@@ -290,11 +293,8 @@
     pair_start(3, 0)
     pair_start(3, 1)
     sib_wait(0)
-    loads["res"].wait()
-    for s in range(2):
-        for l in range(2):
-            for p in range(2):
-                mate_wait(l, s, p)
+    load_wait(resv, 5)
+    mate_wait(0)
     each(0, 1, lambda i: own_product(0, t1, blocks(i)))
     pair_wait(3, 0)
     mate_start(3, 0)
@@ -312,16 +312,12 @@
     sib_start(3, 0)
     each(1, 2, lambda i: nbr_product(0, blocks(i)))
     each(1, 2, lambda i: own_product(0, t1, blocks(i)))
-    for l in range(2):
-        for p in range(2):
-            mate_wait(l, 2, p)
+    mate_wait(1)
     forward_start(2)
     y_wait(2, 1)
     sib_start(2, 1)
     sib_start(2, 2)
-    for l in range(2):
-        for p in range(2):
-            mate_wait(l, 3, p)
+    mate_wait(2)
     for j in range(3, 6):
         forward_start(j)
     each(2, 3, lambda i: nbr_product(0, blocks(i)))
@@ -343,11 +339,10 @@
     @pl.loop(0, 3)
     def _(i):
         for n in blocks(i):
-            out_copy(0, n).wait_recv()
+            out_wait(0, n)
             finish(n, 0, t1)
 
     forward_wait(0)
-    forward_wait(1)
     first, last = blocks(3)
 
     @pl.loop(0, 2)
@@ -355,8 +350,8 @@
         ts = pl.ds(pl.multiple_of(h * ht, ht), ht)
         obuf[first, ts, :] = product(1, ts.start, ht, [first]).astype(BF16)
 
-    for h in range(2):
-        out_copy(h, first).start()
+    for g in range(2):
+        out_start(g, first)
     y_last(3)
     sib_start(3, 3)
     sib_wait(3)
@@ -364,8 +359,7 @@
     y_wait(4, 0)
     y_forward(4)
     each(1, 3, lambda i: own_product(t1, t2 - t1, blocks(i)))
-    forward_wait(2)
-    forward_wait(3)
+    forward_wait(1)
 
     @pl.loop(0, 2)
     def _(h):
@@ -375,53 +369,62 @@
     y_wait(4, 1)
     sib_start(4, 1)
     sib_start(4, 2)
-    forward_wait(4)
-    forward_wait(5)
+    forward_wait(2)
 
     @pl.loop(0, 2)
     def _(h):
         ts = pl.ds(pl.multiple_of(h * ht, ht), ht)
         obuf[last, ts, :] = (early[ts, :] + product(1, ts.start, ht, [last], late, width)).astype(BF16)
 
-    for h in range(2):
-        out_copy(h, last).start()
+    for g in range(2):
+        out_start(g, last)
     y_last(4)
     sib_start(4, 3)
-    pl.loop(0, 2)(lambda i: own_product(pl.multiple_of(i * t1, t1), t1, [first, last]))
+    @pl.loop(0, 2)
+    def _(i):
+        own_product(pl.multiple_of(i * t1, t1), t1, [first, last])
+        for j in range(3):
+            k = 3 * i + j
+            one, other = blocks(k // 2)
+            n = jnp.where(lax.rem(k, 2) == 0, one, other)
+            out_wait(1, n)
+            finish(n, t1, t2 - t1)
+
     sib_wait(4)
     pl.loop(0, 2)(lambda i: own_product(t2, tokens - t2, blocks(2 * i) + blocks(2 * i + 1)))
 
     served = pltpu.make_async_copy(
-        wbuf.at[:, :, :, pl.ds(pl.multiple_of((c // 2) * kh, kh), kh)], served_o, l_sem.at[len(loads)])
+        wbuf.at[:, :, :, pl.ds(pl.multiple_of((c // 2) * kh, kh), kh)], served_o, l_sem.at[6])
     served.start()
 
     @pl.loop(0, 3)
     def _(i):
         for n in blocks(i):
-            out_copy(1, n).wait_recv()
-            finish(n, t1, tokens - t1)
+            finish(n, t2, tokens - t2)
 
     for n in (first, last):
         for g in range(2):
-            out_copy(g, n).wait_recv()
+            out_wait(g, n)
         finish(n, 0, tokens)
 
     for t in range(tokens // 128):
         sums[r, t:t + 1, :] = jnp.sum(squares[t * 128:(t + 1) * 128, :].T, axis=0, keepdims=True)
-    for i, d in enumerate(peers):
-        go(sums.at[r], sums.at[r], q_send.at[i], q_recv.at[i], d)
+    for i in (3, 4, 2, 5, 1, 6, 0):
+        go(sums.at[r], sums.at[r], q_send, q_recv.at[i], peers[i])
+    served.wait()
+    left(wbuf.at[pl.ds(0, 3)], c_send, c_recv.at[0, 0])
+    left(wbuf.at[0, pl.ds(0, 3)], p_send, p_recv.at[0, 0])
+    left(abuf.at[0, 0], n_send, n_recv.at[0])
+    left(abuf.at[0, pl.ds(0, 6)], y_send, y_recv.at[0, 0, 0])
+    left(abuf.at[0], s_send, s_recv.at[0, 0])
+    left(obuf, o_send, o_recv.at[0, 0])
     for i in range(1, NR):
-        arrived(sums.at[lax.rem(r + NR - i, NR)], q_send.at[i - 1], q_recv.at[i - 1], peers[i - 1])
+        arrived(sums.at[lax.rem(r + NR - i, NR)], q_send, q_recv.at[i - 1])
     total = sums[0]
     for i in range(1, NR):
         total = total + sums[i]
     total_o[...] = total
-    served.wait()
-    for n in range(NR):
-        for h in range(2):
-            out_copy(h, n).wait_send()
-    for cp in sent:
-        cp.wait_send()
+    left(sums.at[pl.ds(0, NR - 1)], q_send, q_recv.at[0])
 
 
 def finish(served, hidden, total, gain, served_o, hidden_o, normed_o, normv, sem):
@@ -475,14 +478,14 @@
             pltpu.VMEM((tokens, 2 * rows), F32),
             pltpu.VMEM((tokens, 128), F32),
             pltpu.VMEM((NR, tokens // 128, 128), F32),
-            dma((2, 14)), dma((2, 14)),
-            dma((3, 2)), dma((3, 2)),
-            dma((2,)), dma((2,)),
-            dma((5, 3, 2)), dma((5, 3, 2)),
-            dma((5, 4)), dma((5, 4)),
-            dma((2, NR)), dma((2, NR)),
-            dma((NR - 1,)), dma((NR - 1,)),
-            dma((4 * NR + 3,)),
+            dma(()), dma((2, 14)),
+            dma(()), dma((3, 2)),
+            dma(()), dma((2,)),
+            dma(()), dma((5, 3, 2)),
+            dma(()), dma((5, 4)),
+            dma(()), dma((2, NR)),
+            dma(()), dma((NR - 1,)),
+            dma((7 + 4 * NR,)),
             pltpu.SemaphoreType.REGULAR,
         ],
         compiler_params=pltpu.CompilerParams(

time: 93.6 us -> 92.4 us (0.987)
  Pallas kernels: 92.6 us -> 91.5 us
    pallas_call x1, Pallas kernels: 90.2 us -> 89 us  [per_device(): pl.pallas_call(kernel, out_shape=tuple((pltpu.VMEM(a.shape, a.dtype) for...]
where the time goes in v6:
time: 92.4 us; the launch traced here: 92.3 us
  Pallas kernels  91.5 us (99%)
    pallas_call x1, Pallas kernels, per_device(): pl.pallas_call(kernel, out_shape=tuple((pltpu.VMEM(a.shape, a.dtype) for...  89 us
    pallas_call x1, Pallas kernels, per_device(): pl.pallas_call(finish, out_shape=shapes, in_specs=[vmem] * 4, out_specs=(...  2.41 us

profile of v6, /device:TPU:1, one launch (start us, length us, event | category | flops | bytes accessed | tf_op | source)
XLA Modules:
  0.0 92.3 jit_solution(4346248465940875884)
XLA Ops:
  0.6 0.0 copy-start
  0.6 89.0 %shard_map.67 = (bf16[4,4,64,512]{3,2,1,0:T(8,128)(2,1)S(1)}, bf16[1024,1024]{1,0:T(8,128)(2,1)S(1)}, f32[8,128]{1,0:T(8,128)S(1)}) custom-call(bf16[1024,1024]{1,0:T(8,128)(2,1)} %att.1, bf16[1024,1024]{1,0:T(8,128)(2,1)} %res.1, bf16[64,8192]{1,0:T(8,128)(2,1)} %wsh.1), custom_call_target="tpu_custom_call" | custom-call | flops 17179869184 | bytes 10485760 | tf_op jit(solution)/shard_map/pallas_call | solution.py:465
  89.7 0.0 copy-done
  89.7 2.4 %shard_map.68 = (bf16[4,4,64,512]{3,2,1,0:T(8,128)(2,1)}, bf16[1024,1024]{1,0:T(8,128)(2,1)}, bf16[1024,1024]{1,0:T(8,128)(2,1)}) custom-call(bf16[4,4,64,512]{3,2,1,0:T(8,128)(2,1)S(1)} %get-tuple-element.9.served, bf16[1024,1024]{1,0:T(8,128)(2,1)S(1)} %get-tuple-element.10.hidden, f32[8,128]{1,0:T(8,128)S(1)} %get-tuple-element.11.total, ...), custom_call_target="tpu_custom_call" | custom-call | flops 4194304 | bytes 5242880 | tf_op jit(solution)/shard_map/pallas_call | solution.py:498
Async XLA Ops:
  0.6 89.1 %copy-start = (bf16[1024]{0:T(1024)(128)(2,1)S(1)}, bf16[1024]{0:T(1024)(128)(2,1)}, u32[]{:S(2)}) copy-start(bf16[1024]{0:T(1024)(128)(2,1)} %gain.1) | copy-start | bytes 6148

commit v7 on v6

--- a/solution.py
+++ b/solution.py
@@ -69,18 +69,14 @@
     def load_wait(ref, i):
         pltpu.make_async_copy(ref, ref, l_sem.at[i]).wait()
 
-    def load_waits(ref, i):
-        for k in range(NR):
-            load_wait(ref.at[:, pl.ds(k * kh, kh)], 7 + i * NR + k)
-
     for p in range(2):
         for k in range(NR):
             ps, ks = pl.ds(p * part, part), pl.ds(k * kh, kh)
-            load(wsh.at[ps, cols(k, colour)], wbuf.at[z, x, ps, ks], 7 + p * NR + k)
+            load(wsh.at[ps, cols(k, colour)], wbuf.at[z, x, ps, ks], p)
     for p in range(2):
         for k in range(NR):
             ps, ks = pl.ds(p * part, part), pl.ds(k * kh, kh)
-            load(wsh.at[ps, cols(k, 1 - colour)], wother.at[ps, ks], 7 + (2 + p) * NR + k)
+            load(wsh.at[ps, cols(k, 1 - colour)], wother.at[ps, ks], 2 + p)
     load(att.at[:, my_cols(colour)], abuf.at[0, r], 4)
     load(res, resv, 5)
     pl.semaphore_wait(barrier, len(greeted))
@@ -164,34 +160,29 @@
         for piece in range(2):
             for d in range(2):
                 ref = a_ref(i, y, core, (piece if d == 0 else 1 - piece) * n, n)
-                go(ref, ref, y_send, y_recv.at[i, piece, d], ydev[d])
+                go(ref, ref, y_send, y_recv.at[i, piece], ydev[d])
 
     def y_wait(i, piece):
-        n = chunks[i][2] // 2
-        for d in range(2):
-            ref = a_ref(i, down if d == 0 else up, core, (piece if d == 0 else 1 - piece) * n, n)
-            arrived(ref, y_send, y_recv.at[i, piece, d])
+        arrived(a_ref(i, y, core, 0, chunks[i][2]), y_send, y_recv.at[i, piece])
 
     def y_forward(i):
         n = chunks[i][2] // 2
         for d in range(2):
             ref = a_ref(i, down if d == 0 else up, core, d * n, n)
-            go(ref, ref, y_send, y_recv.at[i, 2, d], ydev[d])
+            go(ref, ref, y_send, y_recv.at[i, 2], ydev[d])
 
     def y_last(i):
-        n = chunks[i][2] // 2
-        for d in range(2):
-            arrived(a_ref(i, across, core, d * n, n), y_send, y_recv.at[i, 2, d])
+        y_wait(i, 2)
 
     ys = [y, up, down, across]
 
     def sib_start(i, j):
         ref = a_ref(i, ys[j], core, 0, chunks[i][2])
-        go(ref, ref, s_send, s_recv.at[i, j], sibling)
+        go(ref, ref, s_send, s_recv.at[i], sibling)
 
     def sib_wait(i):
-        for j in range(4):
-            arrived(a_ref(i, ys[j], 1 - core, 0, chunks[i][2]), s_send, s_recv.at[i, j])
+        o, t0, n = chunks[i]
+        arrived(abuf.at[o, pl.ds(0, 4), pl.ds(t0, n), :], s_send, s_recv.at[i])
 
     nb = 2 * rows
 
@@ -250,14 +241,14 @@
         pl.loop(zero + lo, zero + hi)(f)
 
     for p in range(2):
-        load_waits(wbuf.at[z, x, pl.ds(p * part, part), :], p)
+        load_wait(wbuf.at[z, x, pl.ds(p * part, part), :], p)
         mate_start(0, p)
         if p == 0:
             nbr_start(0)
             load_wait(abuf.at[0, r], 4)
             y_start(0)
     for p in range(2):
-        load_waits(wother.at[pl.ds(p * part, part), :], 2 + p)
+        load_wait(wother.at[pl.ds(p * part, part), :], 2 + p)
         pair_start(1, p)
         pair_start(2, p)
     sib_start(0, 0)
@@ -410,21 +401,20 @@
     for t in range(tokens // 128):
         sums[r, t:t + 1, :] = jnp.sum(squares[t * 128:(t + 1) * 128, :].T, axis=0, keepdims=True)
     for i in (3, 4, 2, 5, 1, 6, 0):
-        go(sums.at[r], sums.at[r], q_send, q_recv.at[i], peers[i])
+        go(sums.at[r], sums.at[r], q_send, q_recv, peers[i])
     served.wait()
     left(wbuf.at[pl.ds(0, 3)], c_send, c_recv.at[0, 0])
     left(wbuf.at[0, pl.ds(0, 3)], p_send, p_recv.at[0, 0])
     left(abuf.at[0, 0], n_send, n_recv.at[0])
-    left(abuf.at[0, pl.ds(0, 6)], y_send, y_recv.at[0, 0, 0])
-    left(abuf.at[0], s_send, s_recv.at[0, 0])
+    left(abuf.at[0, pl.ds(0, 6)], y_send, y_recv.at[0, 0])
+    left(abuf.at[0], s_send, s_recv.at[0])
     left(obuf, o_send, o_recv.at[0, 0])
-    for i in range(1, NR):
-        arrived(sums.at[lax.rem(r + NR - i, NR)], q_send, q_recv.at[i - 1])
+    arrived(sums.at[pl.ds(0, NR - 1)], q_send, q_recv)
     total = sums[0]
     for i in range(1, NR):
         total = total + sums[i]
     total_o[...] = total
-    left(sums.at[pl.ds(0, NR - 1)], q_send, q_recv.at[0])
+    left(sums.at[pl.ds(0, NR - 1)], q_send, q_recv)
 
 
 def finish(served, hidden, total, gain, served_o, hidden_o, normed_o, normv, sem):
@@ -481,11 +471,11 @@
             dma(()), dma((2, 14)),
             dma(()), dma((3, 2)),
             dma(()), dma((2,)),
-            dma(()), dma((5, 3, 2)),
-            dma(()), dma((5, 4)),
+            dma(()), dma((5, 3)),
+            dma(()), dma((5,)),
             dma(()), dma((2, NR)),
-            dma(()), dma((NR - 1,)),
-            dma((7 + 4 * NR,)),
+            dma(()), dma(()),
+            dma((7,)),
             pltpu.SemaphoreType.REGULAR,
         ],
         compiler_params=pltpu.CompilerParams(

time: 92.4 us -> 91.7 us (level)
  no operation moved by 1% of the time
where the time goes in v7:
time: 91.7 us; the launch traced here: 91.6 us
  Pallas kernels  90.8 us (99%)
    pallas_call x1, Pallas kernels, per_device(): pl.pallas_call(kernel, out_shape=tuple((pltpu.VMEM(a.shape, a.dtype) for...  88.4 us
    pallas_call x1, Pallas kernels, per_device(): pl.pallas_call(finish, out_shape=shapes, in_specs=[vmem] * 4, out_specs=(...  2.41 us

profile of v7, /device:TPU:1, one launch (start us, length us, event | category | flops | bytes accessed | tf_op | source)
XLA Modules:
  0.0 91.6 jit_solution(11115515927672740876)
XLA Ops:
  0.6 0.0 copy-start
  0.6 88.4 %shard_map.67 = (bf16[4,4,64,512]{3,2,1,0:T(8,128)(2,1)S(1)}, bf16[1024,1024]{1,0:T(8,128)(2,1)S(1)}, f32[8,128]{1,0:T(8,128)S(1)}) custom-call(bf16[1024,1024]{1,0:T(8,128)(2,1)} %att.1, bf16[1024,1024]{1,0:T(8,128)(2,1)} %res.1, bf16[64,8192]{1,0:T(8,128)(2,1)} %wsh.1), custom_call_target="tpu_custom_call" | custom-call | flops 17179869184 | bytes 10485760 | tf_op jit(solution)/shard_map/pallas_call | solution.py:455
  89.1 0.0 copy-done
  89.1 2.4 %shard_map.68 = (bf16[4,4,64,512]{3,2,1,0:T(8,128)(2,1)}, bf16[1024,1024]{1,0:T(8,128)(2,1)}, bf16[1024,1024]{1,0:T(8,128)(2,1)}) custom-call(bf16[4,4,64,512]{3,2,1,0:T(8,128)(2,1)S(1)} %get-tuple-element.9.served, bf16[1024,1024]{1,0:T(8,128)(2,1)S(1)} %get-tuple-element.10.hidden, f32[8,128]{1,0:T(8,128)S(1)} %get-tuple-element.11.total, ...), custom_call_target="tpu_custom_call" | custom-call | flops 4194304 | bytes 5242880 | tf_op jit(solution)/shard_map/pallas_call | solution.py:488
Async XLA Ops:
  0.6 88.4 %copy-start = (bf16[1024]{0:T(1024)(128)(2,1)S(1)}, bf16[1024]{0:T(1024)(128)(2,1)}, u32[]{:S(2)}) copy-start(bf16[1024]{0:T(1024)(128)(2,1)} %gain.1) | copy-start | bytes 6148

commit v8 on v7

--- a/solution.py
+++ b/solution.py
@@ -114,28 +114,23 @@
     def mate_start(s, p):
         for l in range(2):
             ref = w_ref(z, x, s, p)
-            go(ref, ref, c_send, c_recv.at[l, 2 * s + p], mates[l])
+            go(ref, ref, c_send, c_recv.at[max(s - 1, 0)], mates[l])
 
     def mate_wait(i):
-        for s in ((0, 1), (2,), (3,))[i]:
-            for p in range(2):
-                arrived(w_ref(z, mx, s, p), c_send, c_recv.at[0, 2 * s + p])
-                arrived(w_ref(mz, x, s, p), c_send, c_recv.at[1, 2 * s + p])
+        arrived(wbuf.at[0] if i == 0 else wbuf.at[0, pl.ds(0, 2)], c_send, c_recv.at[i])
 
     pieces = [(0, 0, width), (1, 0, width), (2, 0, late), (3, 0, late), (2, late, width), (3, late, width)]
 
     def forward_start(j):
         s, lo, hi = pieces[j]
         ref = w_ref(z, mx, s, 0, lo, hi)
-        go(ref, ref, c_send, c_recv.at[1, 8 + j], mates[1])
+        go(ref, ref, c_send, c_recv.at[3 + j // 2], mates[1])
         ref = w_ref(mz, x, s, 1, lo, hi)
-        go(ref, ref, c_send, c_recv.at[0, 8 + j], mates[0])
+        go(ref, ref, c_send, c_recv.at[3 + j // 2], mates[0])
 
     def forward_wait(i):
-        for j in (2 * i, 2 * i + 1):
-            s, lo, hi = pieces[j]
-            for l in range(2):
-                arrived(w_ref(mz, mx, s, 1 - l, lo, hi), c_send, c_recv.at[l, 8 + j])
+        _, lo, hi = pieces[2 * i]
+        arrived(wbuf.at[0, pl.ds(0, 2), :, pl.ds(lo, hi - lo)], c_send, c_recv.at[3 + i])
 
     t1, t2 = 3 * tokens // 8, 6 * tokens // 8
     groups = [(0, 8 * tokens // 16), (8 * tokens // 16, 8 * tokens // 16)]
@@ -207,19 +202,19 @@
         a = [abuf[o, k, pl.ds(t0, nt), :] for k in range(lo // kh, hi // kh)]
         return dot(jnp.concatenate(a, axis=1), w[0] if len(w) == 1 else jnp.concatenate(w, axis=0))
 
-    def out_start(g, n):
+    def out_start(g, n, i):
         ts = pl.ds(*groups[g])
-        go(obuf.at[n, ts, :], ibuf.at[n, ts, :], o_send, o_recv.at[g, n], pz_dev if g == 0 else px_dev)
-
-    def out_wait(g, n):
-        arrived(ibuf.at[n, pl.ds(*groups[g]), :], o_send, o_recv.at[g, n])
+        go(obuf.at[n, ts, :], ibuf.at[n, ts, :], o_send, o_recv.at[i], pz_dev if g == 0 else px_dev)
+
+    def out_wait(i):
+        arrived(ibuf.at[pl.ds(0, 6), pl.ds(*groups[i]), :] if i < 2 else ibuf.at[0], o_send, o_recv.at[i])
 
     def nbr_product(g, ns):
         v = product(1, *groups[g], ns).astype(BF16)
         for j, n in enumerate(ns):
             obuf[n, pl.ds(*groups[g]), :] = v[:, j * nb:(j + 1) * nb]
         for n in ns:
-            out_start(g, n)
+            out_start(g, n, g)
 
     def own_product(t0, nt, ns):
         v = product(0, t0, nt, ns)
@@ -327,10 +322,11 @@
     sib_start(3, 2)
     squares[...] = jnp.zeros_like(squares)
 
+    out_wait(0)
+
     @pl.loop(0, 3)
     def _(i):
         for n in blocks(i):
-            out_wait(0, n)
             finish(n, 0, t1)
 
     forward_wait(0)
@@ -341,8 +337,8 @@
         ts = pl.ds(pl.multiple_of(h * ht, ht), ht)
         obuf[first, ts, :] = product(1, ts.start, ht, [first]).astype(BF16)
 
-    for g in range(2):
-        out_start(g, first)
+    out_start(0, first, 3)
+    out_start(1, first, 2)
     y_last(3)
     sib_start(3, 3)
     sib_wait(3)
@@ -363,14 +359,22 @@
     forward_wait(2)
 
     @pl.loop(0, 2)
-    def _(h):
-        ts = pl.ds(pl.multiple_of(h * ht, ht), ht)
+    def _(i):
+        ts = pl.ds(pl.multiple_of((1 - i) * ht, ht), ht)
         obuf[last, ts, :] = (early[ts, :] + product(1, ts.start, ht, [last], late, width)).astype(BF16)
 
-    for g in range(2):
-        out_start(g, last)
+        @pl.when(i == 0)
+        def _():
+            out_start(1, last, 3)
+
+        @pl.when(i == 1)
+        def _():
+            out_start(0, last, 2)
+
     y_last(4)
     sib_start(4, 3)
+    out_wait(1)
+
     @pl.loop(0, 2)
     def _(i):
         own_product(pl.multiple_of(i * t1, t1), t1, [first, last])
@@ -378,7 +382,6 @@
             k = 3 * i + j
             one, other = blocks(k // 2)
             n = jnp.where(lax.rem(k, 2) == 0, one, other)
-            out_wait(1, n)
             finish(n, t1, t2 - t1)
 
     sib_wait(4)
@@ -393,9 +396,8 @@
         for n in blocks(i):
             finish(n, t2, tokens - t2)
 
-    for n in (first, last):
-        for g in range(2):
-            out_wait(g, n)
+    for i, n in ((2, first), (3, last)):
+        out_wait(i)
         finish(n, 0, tokens)
 
     for t in range(tokens // 128):
@@ -403,12 +405,12 @@
     for i in (3, 4, 2, 5, 1, 6, 0):
         go(sums.at[r], sums.at[r], q_send, q_recv, peers[i])
     served.wait()
-    left(wbuf.at[pl.ds(0, 3)], c_send, c_recv.at[0, 0])
+    left(wbuf.at[pl.ds(0, 3)], c_send, c_recv.at[0])
     left(wbuf.at[0, pl.ds(0, 3)], p_send, p_recv.at[0, 0])
     left(abuf.at[0, 0], n_send, n_recv.at[0])
     left(abuf.at[0, pl.ds(0, 6)], y_send, y_recv.at[0, 0])
     left(abuf.at[0], s_send, s_recv.at[0])
-    left(obuf, o_send, o_recv.at[0, 0])
+    left(obuf, o_send, o_recv.at[0])
     arrived(sums.at[pl.ds(0, NR - 1)], q_send, q_recv)
     total = sums[0]
     for i in range(1, NR):
@@ -468,12 +470,12 @@
             pltpu.VMEM((tokens, 2 * rows), F32),
             pltpu.VMEM((tokens, 128), F32),
             pltpu.VMEM((NR, tokens // 128, 128), F32),
-            dma(()), dma((2, 14)),
+            dma(()), dma((6,)),
             dma(()), dma((3, 2)),
             dma(()), dma((2,)),
             dma(()), dma((5, 3)),
             dma(()), dma((5,)),
-            dma(()), dma((2, NR)),
+            dma(()), dma((4,)),
             dma(()), dma(()),
             dma((7,)),
             pltpu.SemaphoreType.REGULAR,

time: 91.7 us -> 91.5 us (level)
  no operation moved by 1% of the time
where the time goes in v8:
time: 91.5 us; the launch traced here: 91.4 us
  Pallas kernels  90.6 us (99%)
    pallas_call x1, Pallas kernels, per_device(): pl.pallas_call(kernel, out_shape=tuple((pltpu.VMEM(a.shape, a.dtype) for...  88.2 us
    pallas_call x1, Pallas kernels, per_device(): pl.pallas_call(finish, out_shape=shapes, in_specs=[vmem] * 4, out_specs=(...  2.41 us

profile of v8, /device:TPU:1, one launch (start us, length us, event | category | flops | bytes accessed | tf_op | source)
XLA Modules:
  0.0 91.4 jit_solution(6032887854925957170)
XLA Ops:
  0.6 0.0 copy-start
  0.6 88.2 %shard_map.67 = (bf16[4,4,64,512]{3,2,1,0:T(8,128)(2,1)S(1)}, bf16[1024,1024]{1,0:T(8,128)(2,1)S(1)}, f32[8,128]{1,0:T(8,128)S(1)}) custom-call(bf16[1024,1024]{1,0:T(8,128)(2,1)} %att.1, bf16[1024,1024]{1,0:T(8,128)(2,1)} %res.1, bf16[64,8192]{1,0:T(8,128)(2,1)} %wsh.1), custom_call_target="tpu_custom_call" | custom-call | flops 17179869184 | bytes 10485760 | tf_op jit(solution)/shard_map/pallas_call | solution.py:457
  88.8 0.0 copy-done
  88.8 2.4 %shard_map.68 = (bf16[4,4,64,512]{3,2,1,0:T(8,128)(2,1)}, bf16[1024,1024]{1,0:T(8,128)(2,1)}, bf16[1024,1024]{1,0:T(8,128)(2,1)}) custom-call(bf16[4,4,64,512]{3,2,1,0:T(8,128)(2,1)S(1)} %get-tuple-element.9.served, bf16[1024,1024]{1,0:T(8,128)(2,1)S(1)} %get-tuple-element.10.hidden, f32[8,128]{1,0:T(8,128)S(1)} %get-tuple-element.11.total, ...), custom_call_target="tpu_custom_call" | custom-call | flops 4194304 | bytes 5242880 | tf_op jit(solution)/shard_map/pallas_call | solution.py:490
Async XLA Ops:
  0.6 88.2 %copy-start = (bf16[1024]{0:T(1024)(128)(2,1)S(1)}, bf16[1024]{0:T(1024)(128)(2,1)}, u32[]{:S(2)}) copy-start(bf16[1024]{0:T(1024)(128)(2,1)} %gain.1) | copy-start | bytes 6148

commit v9 on v8

--- a/solution.py
+++ b/solution.py
@@ -373,19 +373,17 @@
 
     y_last(4)
     sib_start(4, 3)
+    pl.loop(0, 2)(lambda i: own_product(pl.multiple_of(i * t1, t1), t1, [first, last]))
+    sib_wait(4)
     out_wait(1)
 
     @pl.loop(0, 2)
     def _(i):
-        own_product(pl.multiple_of(i * t1, t1), t1, [first, last])
+        own_product(t2, tokens - t2, blocks(2 * i) + blocks(2 * i + 1))
         for j in range(3):
             k = 3 * i + j
             one, other = blocks(k // 2)
-            n = jnp.where(lax.rem(k, 2) == 0, one, other)
-            finish(n, t1, t2 - t1)
-
-    sib_wait(4)
-    pl.loop(0, 2)(lambda i: own_product(t2, tokens - t2, blocks(2 * i) + blocks(2 * i + 1)))
+            finish(jnp.where(lax.rem(k, 2) == 0, one, other), t1, t2 - t1)
 
     served = pltpu.make_async_copy(
         wbuf.at[:, :, :, pl.ds(pl.multiple_of((c // 2) * kh, kh), kh)], served_o, l_sem.at[6])

time: 91.5 us -> 91.5 us (level)
  no operation moved by 1% of the time
where the time goes in v9:
time: 91.5 us; the launch traced here: 91.4 us
  Pallas kernels  90.6 us (99%)
    pallas_call x1, Pallas kernels, per_device(): pl.pallas_call(kernel, out_shape=tuple((pltpu.VMEM(a.shape, a.dtype) for...  88.2 us
    pallas_call x1, Pallas kernels, per_device(): pl.pallas_call(finish, out_shape=shapes, in_specs=[vmem] * 4, out_specs=(...  2.41 us

profile of v9, /device:TPU:1, one launch (start us, length us, event | category | flops | bytes accessed | tf_op | source)
XLA Modules:
  0.0 91.4 jit_solution(14052470177330549045)
XLA Ops:
  0.6 0.0 copy-start
  0.6 88.2 %shard_map.67 = (bf16[4,4,64,512]{3,2,1,0:T(8,128)(2,1)S(1)}, bf16[1024,1024]{1,0:T(8,128)(2,1)S(1)}, f32[8,128]{1,0:T(8,128)S(1)}) custom-call(bf16[1024,1024]{1,0:T(8,128)(2,1)} %att.1, bf16[1024,1024]{1,0:T(8,128)(2,1)} %res.1, bf16[64,8192]{1,0:T(8,128)(2,1)} %wsh.1), custom_call_target="tpu_custom_call" | custom-call | flops 17179869184 | bytes 10485760 | tf_op jit(solution)/shard_map/pallas_call | solution.py:455
  88.8 0.0 copy-done
  88.8 2.4 %shard_map.68 = (bf16[4,4,64,512]{3,2,1,0:T(8,128)(2,1)}, bf16[1024,1024]{1,0:T(8,128)(2,1)}, bf16[1024,1024]{1,0:T(8,128)(2,1)}) custom-call(bf16[4,4,64,512]{3,2,1,0:T(8,128)(2,1)S(1)} %get-tuple-element.9.served, bf16[1024,1024]{1,0:T(8,128)(2,1)S(1)} %get-tuple-element.10.hidden, f32[8,128]{1,0:T(8,128)S(1)} %get-tuple-element.11.total, ...), custom_call_target="tpu_custom_call" | custom-call | flops 4194304 | bytes 5242880 | tf_op jit(solution)/shard_map/pallas_call | solution.py:488
Async XLA Ops:
  0.6 88.2 %copy-start = (bf16[1024]{0:T(1024)(128)(2,1)S(1)}, bf16[1024]{0:T(1024)(128)(2,1)}, u32[]{:S(2)}) copy-start(bf16[1024]{0:T(1024)(128)(2,1)} %gain.1) | copy-start | bytes 6148

commit v10 on v9

--- a/solution.py
+++ b/solution.py
@@ -132,7 +132,7 @@
         _, lo, hi = pieces[2 * i]
         arrived(wbuf.at[0, pl.ds(0, 2), :, pl.ds(lo, hi - lo)], c_send, c_recv.at[3 + i])
 
-    t1, t2 = 3 * tokens // 8, 6 * tokens // 8
+    t1, t2 = 3 * tokens // 8, 13 * tokens // 16
     groups = [(0, 8 * tokens // 16), (8 * tokens // 16, 8 * tokens // 16)]
     chunks = [(0, 0, t1), (1, *groups[0]), (1, *groups[1]), (0, t1, t2 - t1), (0, t2, tokens - t2)]
 
@@ -373,7 +373,7 @@
 
     y_last(4)
     sib_start(4, 3)
-    pl.loop(0, 2)(lambda i: own_product(pl.multiple_of(i * t1, t1), t1, [first, last]))
+    pl.loop(0, 2)(lambda i: own_product(pl.multiple_of(i * (t2 // 2), t2 // 2), t2 // 2, [first, last]))
     sib_wait(4)
     out_wait(1)
 

time: 91.5 us -> 91.8 us (level)
  no operation moved by 1% of the time
where the time goes in v10:
time: 91.8 us; the launch traced here: 91.7 us
  Pallas kernels  90.9 us (99%)
    pallas_call x1, Pallas kernels, per_device(): pl.pallas_call(kernel, out_shape=tuple((pltpu.VMEM(a.shape, a.dtype) for...  88.5 us
    pallas_call x1, Pallas kernels, per_device(): pl.pallas_call(finish, out_shape=shapes, in_specs=[vmem] * 4, out_specs=(...  2.41 us

profile of v10, /device:TPU:1, one launch (start us, length us, event | category | flops | bytes accessed | tf_op | source)
XLA Modules:
  0.0 91.7 jit_solution(12475461843652407565)
XLA Ops:
  0.6 0.0 copy-start
  0.6 88.5 %shard_map.67 = (bf16[4,4,64,512]{3,2,1,0:T(8,128)(2,1)S(1)}, bf16[1024,1024]{1,0:T(8,128)(2,1)S(1)}, f32[8,128]{1,0:T(8,128)S(1)}) custom-call(bf16[1024,1024]{1,0:T(8,128)(2,1)} %att.1, bf16[1024,1024]{1,0:T(8,128)(2,1)} %res.1, bf16[64,8192]{1,0:T(8,128)(2,1)} %wsh.1), custom_call_target="tpu_custom_call" | custom-call | flops 17179869184 | bytes 10485760 | tf_op jit(solution)/shard_map/pallas_call | solution.py:455
  89.2 0.0 copy-done
  89.2 2.4 %shard_map.68 = (bf16[4,4,64,512]{3,2,1,0:T(8,128)(2,1)}, bf16[1024,1024]{1,0:T(8,128)(2,1)}, bf16[1024,1024]{1,0:T(8,128)(2,1)}) custom-call(bf16[4,4,64,512]{3,2,1,0:T(8,128)(2,1)S(1)} %get-tuple-element.9.served, bf16[1024,1024]{1,0:T(8,128)(2,1)S(1)} %get-tuple-element.10.hidden, f32[8,128]{1,0:T(8,128)S(1)} %get-tuple-element.11.total, ...), custom_call_target="tpu_custom_call" | custom-call | flops 4194304 | bytes 5242880 | tf_op jit(solution)/shard_map/pallas_call | solution.py:488
Async XLA Ops:
  0.6 88.5 %copy-start = (bf16[1024]{0:T(1024)(128)(2,1)S(1)}, bf16[1024]{0:T(1024)(128)(2,1)}, u32[]{:S(2)}) copy-start(bf16[1024]{0:T(1024)(128)(2,1)} %gain.1) | copy-start | bytes 6148
